TPU v7x, 256 devices: a whole 4x4x8 slice. The times are simulated.
256 devices in a mesh: gx: 32 (over y, z_lo, x), gy: 8 (over z_hi, core).
Axes of the slice: x: 4, y: 4, z: 8 (z_hi: 4, z_lo: 2; z = z_hi * 2 + z_lo), core: 2. Of those that a mesh axis runs over, the one named last changes fastest.
Arguments:
- node_latents: bfloat16 [32, 8, 256, 512], P('gx', 'gy'), may hold values from -6 to 6
- edge_latents: bfloat16 [32, 8, 768, 512], P('gx', 'gy'), may hold values from -6 to 6
- edge_w1: bfloat16 [1536, 512], replicated, may hold values from -0.15625 to 0.15625
- edge_b1: float32 [512], replicated, may hold values from -3 to 3
- edge_w2: bfloat16 [512, 512], replicated, may hold values from -0.25 to 0.25
- node_w1: bfloat16 [1024, 512], replicated, may hold values from -0.1875 to 0.1875
- node_b1: float32 [512], replicated, may hold values from -3 to 3
- node_w2: bfloat16 [512, 512], replicated, may hold values from -0.25 to 0.25
- node_cot: bfloat16 [32, 8, 256, 512], P('gx', 'gy'), may hold values from -6 to 6
- edge_cot: bfloat16 [32, 8, 768, 512], P('gx', 'gy'), may hold values from -6 to 6
- send_count: int32 [32, 8, 4], P('gx', 'gy'), may hold values from 0 to 2, as said below
- send_list: int32 [32, 8, 4, 2], P('gx', 'gy'), may hold values from 0 to 1
- tile_recv: int32 [32, 8, 6], P('gx', 'gy'), may hold values from 0 to 1
- tile_send: int32 [32, 8, 6], P('gx', 'gy'), may hold values from 0 to 9, as said below
- tile_perm: int32 [32, 8, 6, 128], P('gx', 'gy'), may hold values from 0 to 127, each once within a row
Outputs:
- node_out: bfloat16 [32, 8, 256, 512], P('gx', 'gy')
- node_grad: bfloat16 [32, 8, 256, 512], P('gx', 'gy')
- edge_grad: bfloat16 [32, 8, 768, 512], P('gx', 'gy')
- weight_dir: bfloat16 [1835008], P(('gx', 'gy'))
Inputs may be any that keep to these rules, and one draw needn't show every extreme that they name: `send_count`: entries for a neighbour outside the grid of partitions are 0, all others at least 1; the partition at (0, 0) sends 2 blocks to its neighbour at gx+1. `tile_send`: A value of 2 or more is a halo slot 2 + d * 2 + s that direction d's neighbour fills (s below its send count).
All inputs are finite; a program needn't handle non-finite values.
Results may differ from a plain program's by a relative error of at most 0.0075.
Values may be sent and summed in bfloat16 or wider, within the bound.
A program may use at most 128 MiB of HBM per device.

v0:
```python
import jax
import jax.numpy as jnp
from jax import lax
from jax.sharding import PartitionSpec as P


def padded(block, sides, width):
    for axis, dim in sides:
        count = lax.axis_size(axis)
        forward = [(i, i + 1) for i in range(count - 1)]
        backward = [(target, source) for source, target in forward]
        low = lax.ppermute(
            lax.slice_in_dim(block, block.shape[dim] - width, None, axis=dim), axis, forward
        )
        high = lax.ppermute(lax.slice_in_dim(block, 0, width, axis=dim), axis, backward)
        block = jnp.concatenate([low, block, high], axis=dim)
    return block


def silu_slope(values):
    logistic = jax.nn.sigmoid(values)
    return logistic * (1.0 + values * (1.0 - logistic))


def layer_norm(values):
    center = values - jnp.mean(values, axis=-1, keepdims=True)
    inverse_rms = lax.rsqrt(jnp.mean(center * center, axis=-1, keepdims=True) + 1e-05)
    return (center * inverse_rms, inverse_rms)


def norm_back(normed, inverse_rms, upstream):
    return inverse_rms * (
        upstream
        - jnp.mean(upstream, axis=-1, keepdims=True)
        - normed * jnp.mean(upstream * normed, axis=-1, keepdims=True)
    )


def inner_rows(factor, second):
    return lax.dot_general(
        factor, second, (((0,), (0,)), ((), ())), preferred_element_type=jnp.float32
    )


def times_transposed(factor, second):
    return lax.dot_general(
        factor, second, (((1,), (1,)), ((), ())), preferred_element_type=jnp.float32
    )


def matmul(factor, second):
    return jnp.dot(factor, second, preferred_element_type=jnp.float32)


def fetch_halo(packed):
    row_halo = padded(jnp.stack([packed[1], packed[0]]), (("gx", 0),), 1)
    col_halo = padded(jnp.stack([packed[3], packed[2]]), (("gy", 0),), 1)
    return jnp.concatenate([row_halo[0], row_halo[3], col_halo[0], col_halo[3]], axis=0)


def return_partials(halo_part):
    row_back = padded(
        jnp.stack([halo_part[0], halo_part[1]]).astype(jnp.bfloat16), (("gx", 0),), 1
    ).astype(jnp.float32)
    col_back = padded(
        jnp.stack([halo_part[2], halo_part[3]]).astype(jnp.bfloat16), (("gy", 0),), 1
    ).astype(jnp.float32)
    return jnp.stack([row_back[3], row_back[0], col_back[3], col_back[0]])


def on_device(
    node_latents,
    edge_latents,
    edge_w1,
    edge_b1,
    edge_w2,
    node_w1,
    node_b1,
    node_w2,
    node_cot,
    edge_cot,
    send_count,
    send_list,
    tile_recv,
    tile_send,
    tile_perm,
):
    feature = node_latents.shape[3]
    block_size = tile_perm.shape[3]
    tile_count = tile_perm.shape[2]
    slot_count = send_list.shape[3]
    node_count = node_latents.shape[2]
    block_count = node_count // block_size
    node_blocks = node_latents.reshape(block_count, block_size, feature)
    local_rows = node_latents.reshape(node_count, feature)
    edge_rows = edge_latents.reshape(tile_count * block_size, feature)
    cot_node = node_cot.reshape(node_count, feature)
    cot_edge = edge_cot.reshape(tile_count * block_size, feature)
    send_counts = send_count.reshape(4)
    send_lists = send_list.reshape(4, slot_count)
    recv_idx = tile_recv.reshape(tile_count)
    send_idx = tile_send.reshape(tile_count)
    perm_idx = tile_perm.reshape(tile_count, block_size)
    live_slots = jnp.arange(slot_count, dtype=jnp.int32)[None, :] < send_counts[:, None]
    packed = jnp.where(
        live_slots[:, :, None, None], node_blocks[send_lists], jnp.zeros((), jnp.bfloat16)
    )
    offsets = jnp.arange(block_size, dtype=jnp.int32)
    recv_rows = (recv_idx[:, None] * block_size + offsets[None, :]).reshape(-1)
    send_rows = (send_idx[:, None] * block_size + perm_idx).reshape(-1)
    h_recv = local_rows[recv_rows]
    halo_blocks = fetch_halo(packed)
    flat_ext = jnp.concatenate([node_blocks, halo_blocks], axis=0).reshape(-1, feature)
    h_send = flat_ext[send_rows]
    joined = jnp.concatenate([edge_rows, h_recv, h_send], axis=1)
    edge_affine = matmul(joined, edge_w1) + edge_b1
    edge_hidden = jax.nn.silu(edge_affine).astype(jnp.bfloat16)
    edge_linear = matmul(edge_hidden, edge_w2)
    message, edge_inv = layer_norm(edge_linear)
    recv_hot = (recv_idx[None, :] == jnp.arange(block_count, dtype=jnp.int32)[:, None]).astype(
        jnp.float32
    )
    aggregate = jnp.einsum(
        "bt,tnf->bnf",
        recv_hot,
        message.reshape(tile_count, block_size, feature),
        precision=lax.Precision.HIGHEST,
    )
    aggregate = aggregate.reshape(node_count, feature).astype(jnp.bfloat16)
    node_input = jnp.concatenate([local_rows, aggregate], axis=1)
    node_affine = matmul(node_input, node_w1) + node_b1
    node_hidden = jax.nn.silu(node_affine).astype(jnp.bfloat16)
    node_linear = matmul(node_hidden, node_w2)
    node_normed, node_inv = layer_norm(node_linear)
    node_out = (local_rows.astype(jnp.float32) + node_normed).astype(jnp.bfloat16)
    grad_node_linear = norm_back(node_normed, node_inv, cot_node.astype(jnp.float32)).astype(
        jnp.bfloat16
    )
    g_nw2 = inner_rows(node_hidden, grad_node_linear)
    grad_node_affine = (
        times_transposed(grad_node_linear, node_w2) * silu_slope(node_affine)
    ).astype(jnp.bfloat16)
    g_nw1 = inner_rows(node_input, grad_node_affine)
    grad_node_input = times_transposed(grad_node_affine, node_w1)
    grad_direct = grad_node_input[:, :feature]
    grad_aggregate = grad_node_input[:, feature:]
    grad_message = grad_aggregate[recv_rows] + cot_edge.astype(jnp.float32)
    grad_edge_linear = norm_back(message, edge_inv, grad_message).astype(jnp.bfloat16)
    g_ew2 = inner_rows(edge_hidden, grad_edge_linear)
    grad_edge_affine = (
        times_transposed(grad_edge_linear, edge_w2) * silu_slope(edge_affine)
    ).astype(jnp.bfloat16)
    g_ew1 = inner_rows(joined, grad_edge_affine)
    grad_joined = times_transposed(grad_edge_affine, edge_w1)
    grad_e = grad_joined[:, :feature]
    grad_r = grad_joined[:, feature : 2 * feature]
    grad_s = grad_joined[:, 2 * feature :]
    edge_grad = (cot_edge.astype(jnp.float32) + grad_e).astype(jnp.bfloat16)
    grad_recv = jnp.einsum(
        "bt,tnf->bnf",
        recv_hot,
        grad_r.reshape(tile_count, block_size, feature),
        precision=lax.Precision.HIGHEST,
    )
    inverse = jnp.argsort(perm_idx, axis=1)
    grad_send = jnp.take_along_axis(
        grad_s.reshape(tile_count, block_size, feature), inverse[:, :, None], axis=1
    )
    extended_count = block_count + 4 * slot_count
    send_hot = (send_idx[None, :] == jnp.arange(extended_count, dtype=jnp.int32)[:, None]).astype(
        jnp.float32
    )
    partial_sum = jnp.einsum("bt,tnf->bnf", send_hot, grad_send, precision=lax.Precision.HIGHEST)
    owned_part = (
        partial_sum[:block_count]
        + grad_recv
        + grad_direct.reshape(block_count, block_size, feature)
    )
    halo_part = partial_sum[block_count:].reshape(4, slot_count, block_size, feature)
    returned = return_partials(halo_part)
    back_hot = (
        (send_lists[:, :, None] == jnp.arange(block_count, dtype=jnp.int32)[None, None, :])
        & live_slots[:, :, None]
    ).astype(jnp.float32)
    contrib = jnp.einsum("qsb,qsnf->bnf", back_hot, returned, precision=lax.Precision.HIGHEST)
    node_grad = (
        cot_node.reshape(block_count, block_size, feature).astype(jnp.float32)
        + owned_part
        + contrib
    )
    node_grad = node_grad.astype(jnp.bfloat16).reshape(1, 1, node_count, feature)
    weight_grad = jnp.concatenate([g_ew1, g_ew2, g_nw1, g_nw2], axis=0)
    total_entries = 7 * feature * feature
    share_len = total_entries // lax.axis_size(("gx", "gy"))
    summed = lax.psum(weight_grad, ("gx", "gy"))
    bounds = [0, 3 * feature, 4 * feature, 6 * feature, 7 * feature]
    pieces = []
    for index in range(4):
        matrix = summed[bounds[index] : bounds[index + 1]]
        pieces.append(matrix * lax.rsqrt(jnp.mean(matrix * matrix) + 1e-06))
    normalized = jnp.concatenate(pieces, axis=0).reshape(total_entries)
    own_start = lax.axis_index(("gx", "gy")) * share_len
    weight_dir = lax.dynamic_slice_in_dim(normalized, own_start, share_len).astype(jnp.bfloat16)
    return (
        node_out.reshape(1, 1, node_count, feature),
        node_grad,
        edge_grad.reshape(1, 1, tile_count * block_size, feature),
        weight_dir,
    )


def solution(mesh):
    placed = (
        P("gx", "gy", None, None),
        P("gx", "gy", None, None),
        P(),
        P(),
        P(),
        P(),
        P(),
        P(),
        P("gx", "gy", None, None),
        P("gx", "gy", None, None),
        P("gx", "gy", None),
        P("gx", "gy", None, None),
        P("gx", "gy", None),
        P("gx", "gy", None),
        P("gx", "gy", None, None),
    )
    return jax.shard_map(
        on_device,
        mesh=mesh,
        in_specs=placed,
        out_specs=(
            P("gx", "gy", None, None),
            P("gx", "gy", None, None),
            P("gx", "gy", None, None),
            P(("gx", "gy")),
        ),
        check_vma=False,
    )
```

profile of v0, /device:TPU:1, one launch (start us, length us, event | category | flops | bytes accessed | tf_op | source)
XLA Modules:
  0.0 379.2 jit_solution(667134768034505007)
XLA Ops:
  8.1 0.8 compare_select_fusion.3
  9.0 0.7 iota_compare_fusion.1
  9.8 1.6 gather_fusion.1
  11.6 1.0 fusion.59
  12.6 4.6 %collective-permute-start = (bf16[1,2,128,512]{3,2,1,0:T(8,128)(2,1)}, bf16[1,2,128,512]{3,2,1,0:T(8,128)(2,1)}, u32[]{:S(2)}, u32[]{:S(2)}) collective-permute-start(bf16[1,2,128,512]{3,2,1,0:T(8,128)(2,1)} %get-tuple-element.28), channel_id=1, source_target_pairs={{0,8},{8,16},{16,24},{24,32},{32,40},{40,48},{48,56},{56,64},{64,7... | collective-permute-start | bytes 786440 | tf_op jit(solution)/shard_map/ppermute | solution.py:12
  17.2 1.3 collective-permute-start.1
  18.5 5.7 %collective-permute-start.2 = (bf16[1,2,128,512]{3,2,1,0:T(8,128)(2,1)}, bf16[1,2,128,512]{3,2,1,0:T(8,128)(2,1)}, u32[]{:S(2)}, u32[]{:S(2)}) collective-permute-start(bf16[1,2,128,512]{3,2,1,0:T(8,128)(2,1)} %get-tuple-element.26), channel_id=1, source_target_pairs={{0,1},{1,2},{2,3},{3,4},{4,5},{5,6},{6,7},{8,9},{9,10},{10,11},{11... | collective-permute-start | bytes 786440 | tf_op jit(solution)/shard_map/ppermute | solution.py:12
  24.2 1.9 collective-permute-start.3
  26.2 0.6 copy.83
  26.8 0.6 iota.34
  27.8 3.4 gather_fusion
  31.2 1.0 bitcast_dynamic-update-slice_fusion.3
  32.2 1.0 bitcast_dynamic-update-slice_fusion.2
  33.2 1.0 bitcast_dynamic-update-slice_fusion.1
  34.2 1.0 bitcast_dynamic-update-slice_fusion
  35.1 3.3 gather_fusion.2
  38.5 4.3 %multiply_convert_fusion.2 = (bf16[768,512]{1,0:T(8,128)(2,1)S(1)}, f32[768,512]{1,0:T(8,128)}) fusion(f32[512]{0:T(512)S(1)} %copy-done.26, bf16[1536,512]{1,0:T(8,128)(2,1)S(1)} %copy-done, bf16[768,512]{1,0:T(8,128)(2,1)} %gather_fusion.2, bf16[768,512]{1,0:T(8,128)(2,1)} %gather_fusion, bf16[768,512]{1,0:T(8,128)(2,1)} %bitcast.150), kind=kOutput, calls=%fused_computation.28 | convolution fusion | flops 1217396736 | bytes 6293504 | tf_op jit(solution)/shard_map/dot_general | solution.py:52
  42.8 0.6 fusion.60
  44.1 0.5 copy-done.2
  44.6 1.9 fusion.12
  47.0 0.5 copy-done.24
  48.2 0.9 fusion.28
  49.1 1.5 fusion.54
  50.6 0.5 fusion.11
  51.1 0.5 fusion.63
  51.6 1.8 fusion.29
  53.4 0.9 fusion.58
  54.3 3.2 gather_fusion.3
  57.5 2.7 fusion.20
  60.3 0.5 multiply_convert_fusion.1
  60.8 0.6 copy-done.10
  61.4 0.6 fusion.65
  62.4 0.5 copy-done.27
  63.0 0.9 multiply_convert_fusion
  64.6 1.4 fusion.17
  66.4 3.4 pad_maximum_fusion
  69.9 0.7 compare_and_fusion
  70.7 0.7 fusion.33
  71.4 1.4 fusion.64
  72.8 1.9 fusion.19
  74.7 7.8 %gather_fusion.4 = f32[768,512]{1,0:T(8,128)} fusion(f32[6,128,512]{2,1,0:T(8,128)S(1)} %bitcast.133, s32[768]{0:T(1024)S(1)} %fusion.33), kind=kCustom, calls=%fused_computation.4 | custom fusion | bytes 3151872 | tf_op jit(solution)/shard_map/jit(take_along_axis)/gather | solution.py:166
  82.6 4.7 %fusion.62 = (bf16[10,128,512]{2,0,1:T(8,128)(2,1)S(1)}, f32[10,128,512]{2,0,1:T(8,128)S(1)}) fusion(f32[6,128,512]{2,1,0:T(8,128)} %bitcast.137, pred[6,128]{0,1:T(8,128)(4,1)S(1)} %copy.42, s32[6]{0:T(128)S(1)} %bitcast.149), kind=kOutput, calls=%fused_computation.139 | convolution fusion | flops 48234556 | bytes 5505816 | tf_op jit(solution)/shard_map/bt,tnf->bnf/dot_general | solution.py:173
  87.3 0.8 slice_bitcast_fusion.3
  88.1 6.1 %collective-permute-start.4 = (bf16[1,2,128,512]{3,1,2,0:T(2,128)(2,1)S(1)}, bf16[1,2,128,512]{3,1,2,0:T(2,128)(2,1)S(1)}, u32[]{:S(2)}, u32[]{:S(2)}) collective-permute-start(bf16[1,2,128,512]{3,1,2,0:T(2,128)(2,1)S(1)} %get-tuple-element.15), channel_id=1, source_target_pairs={{0,8},{8,16},{16,24},{24,32},{32,40},{40,48},{48,56},{56,64},{64,7... | collective-permute-start | bytes 786440 | tf_op jit(solution)/shard_map/ppermute | solution.py:12
  94.3 1.3 collective-permute-start.5
  95.6 3.0 collective-permute-start.6
  98.5 2.1 collective-permute-start.7
  100.7 1.9 fusion.2
  103.0 0.6 maximum_convert_fusion.1
  103.6 7.7 %collective-permute-done.7 = bf16[1,2,128,512]{3,1,2,0:T(2,128)(2,1)S(1)} collective-permute-done((bf16[1,2,128,512]{3,1,2,0:T(2,128)(2,1)S(1)}, bf16[1,2,128,512]{3,1,2,0:T(2,128)(2,1)S(1)}, u32[]{:S(2)}, u32[]{:S(2)}) %collective-permute-start.7) | collective-permute-done | bytes 262176 | tf_op jit(solution)/shard_map/ppermute | solution.py:15
  111.4 0.6 maximum_convert_fusion
  112.0 1.1 pad_maximum_fusion.2
  113.2 3.2 fusion.8
  116.4 1.0 fusion.24
  117.4 233.8 %all-reduce.2.cloned.1.call-done = f32[3584,512]{1,0:T(8,128)} async-done(((f32[3584,512]{1,0:T(8,128)}), f32[3584,512]{1,0:T(8,128)}) %all-reduce.2.cloned.1.call-update) | async-done | bytes 7340048 | tf_op jit(solution)/shard_map/psum | solution.py:195
  351.3 3.3 multiply_reduce_fusion
  355.2 2.7 multiply_reduce_fusion.1
  358.7 2.5 multiply_reduce_fusion.5
  362.6 2.3 slice_multiply_fusion
  364.9 1.9 slice_multiply_fusion.1
  366.8 1.8 slice_multiply_fusion.3
  368.6 0.7 maximum_bitcast_fusion
  369.3 1.9 copy.54
  371.2 0.6 dynamic_slice.5
  (94 shorter events, 4.9 us)
Async XLA Ops:
  8.0 30.5 %copy-start = (bf16[1536,512]{1,0:T(8,128)(2,1)S(1)}, bf16[1536,512]{1,0:T(8,128)(2,1)}, u32[]{:S(2)}) copy-start(bf16[1536,512]{1,0:T(8,128)(2,1)} %param.17) | copy-start | bytes 4718596
  8.0 61.9 %sort.19.cloned.1.call-start = ((), (), s32[]{:S(2)}) async-start(), calls=%async_computation.1 | async-start | bytes 24608 | tf_op jit(solution)/shard_map/jit(argsort)/sort | solution.py:165
  11.5 14.7 %copy-start.19 = (s32[1,1,6,128]{3,1,2,0:T(1,128)S(1)}, s32[1,1,6,128]{3,1,2,0:T(1,128)}, u32[]{:S(2)}) copy-start(s32[1,1,6,128]{3,1,2,0:T(1,128)} %param.29) | copy-start | bytes 9220
  11.5 15.9 %copy-start.21 = (s32[1,1,6]{2,1,0:T(1,128)S(1)}, s32[1,1,6]{2,1,0:T(1,128)}, u32[]{:S(2)}) copy-start(s32[1,1,6]{2,1,0:T(1,128)} %param.27) | copy-start | bytes 76
  11.6 16.0 %copy-start.22 = (s32[1,1,6]{2,1,0:T(1,128)S(1)}, s32[1,1,6]{2,1,0:T(1,128)}, u32[]{:S(2)}) copy-start(s32[1,1,6]{2,1,0:T(1,128)} %param.28) | copy-start | bytes 76
  11.6 16.1 %copy-start.11 = (bf16[1,1,256,512]{3,2,1,0:T(8,128)(2,1)S(1)}, bf16[1,1,256,512]{3,2,1,0:T(8,128)(2,1)}, u32[]{:S(2)}) copy-start(bf16[1,1,256,512]{3,2,1,0:T(8,128)(2,1)} %param.23) | copy-start | bytes 786436
  11.6 16.2 %copy-start.1 = (bf16[1,1,256,512]{3,2,1,0:T(8,128)(2,1)S(1)}, bf16[1,1,256,512]{3,2,1,0:T(8,128)(2,1)}, u32[]{:S(2)}) copy-start(bf16[1,1,256,512]{3,2,1,0:T(8,128)(2,1)} %param.15) | copy-start | bytes 786436
  12.6 18.6 %collective-permute-start = (bf16[1,2,128,512]{3,2,1,0:T(8,128)(2,1)}, bf16[1,2,128,512]{3,2,1,0:T(8,128)(2,1)}, u32[]{:S(2)}, u32[]{:S(2)}) collective-permute-start(bf16[1,2,128,512]{3,2,1,0:T(8,128)(2,1)} %get-tuple-element.28), channel_id=1, source_target_pairs={{0,8},{8,16},{16,24},{24,32},{32,40},{40,48},{48,56},{56,64},{64,7... | collective-permute-start | bytes 786440 | tf_op jit(solution)/shard_map/ppermute | solution.py:12
  17.2 15.0 %collective-permute-start.1 = (bf16[1,2,128,512]{3,2,1,0:T(8,128)(2,1)}, bf16[1,2,128,512]{3,2,1,0:T(8,128)(2,1)}, u32[]{:S(2)}, u32[]{:S(2)}) collective-permute-start(bf16[1,2,128,512]{3,2,1,0:T(8,128)(2,1)} %get-tuple-element.27), channel_id=1, source_target_pairs={{8,0},{16,8},{24,16},{32,24},{40,32},{48,40},{56,48},{64,56},{72,6... | collective-permute-start | bytes 786440 | tf_op jit(solution)/shard_map/ppermute | solution.py:15
  18.5 14.7 %collective-permute-start.2 = (bf16[1,2,128,512]{3,2,1,0:T(8,128)(2,1)}, bf16[1,2,128,512]{3,2,1,0:T(8,128)(2,1)}, u32[]{:S(2)}, u32[]{:S(2)}) collective-permute-start(bf16[1,2,128,512]{3,2,1,0:T(8,128)(2,1)} %get-tuple-element.26), channel_id=1, source_target_pairs={{0,1},{1,2},{2,3},{3,4},{4,5},{5,6},{6,7},{8,9},{9,10},{10,11},{11... | collective-permute-start | bytes 786440 | tf_op jit(solution)/shard_map/ppermute | solution.py:12
  24.2 9.9 %collective-permute-start.3 = (bf16[1,2,128,512]{3,2,1,0:T(8,128)(2,1)}, bf16[1,2,128,512]{3,2,1,0:T(8,128)(2,1)}, u32[]{:S(2)}, u32[]{:S(2)}) collective-permute-start(bf16[1,2,128,512]{3,2,1,0:T(8,128)(2,1)} %get-tuple-element.25), channel_id=1, source_target_pairs={{1,0},{2,1},{3,2},{4,3},{5,4},{6,5},{7,6},{9,8},{10,9},{11,10},{12... | collective-permute-start | bytes 786440 | tf_op jit(solution)/shard_map/ppermute | solution.py:15
  27.4 323.9 %all-reduce.2.cloned.1.call-start = ((), (), s32[]{:S(2)}) async-start(), calls=%async_computation | async-start | bytes 14680064 | tf_op jit(solution)/shard_map/psum | solution.py:195
  35.1 3.3 copy-start.26
  38.5 4.3 %copy-start.17 = (bf16[512,512]{1,0:T(8,128)(2,1)S(1)}, bf16[512,512]{1,0:T(8,128)(2,1)}, u32[]{:S(2)}) copy-start(bf16[512,512]{1,0:T(8,128)(2,1)} %param.19) | copy-start | bytes 1572868
  42.8 1.0 copy-start.9
  43.5 1.1 copy-start.2
  44.6 2.0 copy-start.14
  44.6 2.0 copy-start.25
  46.5 1.0 copy-start.24
  54.3 3.2 copy-start.7
  57.4 2.7 copy-start.3
  57.4 2.8 copy-start.4
  60.3 1.1 copy-start.10
  61.4 1.0 copy-start.18
  61.4 1.6 copy-start.27
  63.0 1.1 copy-start.15
  63.0 1.4 copy-start.16
  63.0 1.6 copy-start.23
  64.6 1.6 copy-start.6
  64.6 1.9 copy-start.13
  71.4 1.4 copy-start.8
  87.3 13.4 %copy-start.5 = (f32[768,512]{1,0:T(8,128)S(1)}, f32[768,512]{1,0:T(8,128)}, u32[]{:S(2)}) copy-start(f32[768,512]{1,0:T(8,128)} %get-tuple-element.13) | copy-start | bytes 4718596
  88.1 14.7 %collective-permute-start.4 = (bf16[1,2,128,512]{3,1,2,0:T(2,128)(2,1)S(1)}, bf16[1,2,128,512]{3,1,2,0:T(2,128)(2,1)S(1)}, u32[]{:S(2)}, u32[]{:S(2)}) collective-permute-start(bf16[1,2,128,512]{3,1,2,0:T(2,128)(2,1)S(1)} %get-tuple-element.15), channel_id=1, source_target_pairs={{0,8},{8,16},{16,24},{24,32},{32,40},{40,48},{48,56},{56,64},{64,7... | collective-permute-start | bytes 786440 | tf_op jit(solution)/shard_map/ppermute | solution.py:12
  94.3 8.7 %collective-permute-start.5 = (bf16[1,2,128,512]{3,1,2,0:T(2,128)(2,1)S(1)}, bf16[1,2,128,512]{3,1,2,0:T(2,128)(2,1)S(1)}, u32[]{:S(2)}, u32[]{:S(2)}) collective-permute-start(bf16[1,2,128,512]{3,1,2,0:T(2,128)(2,1)S(1)} %get-tuple-element.18), channel_id=1, source_target_pairs={{8,0},{16,8},{24,16},{32,24},{40,32},{48,40},{56,48},{64,56},{72,6... | collective-permute-start | bytes 786440 | tf_op jit(solution)/shard_map/ppermute | solution.py:15
  95.6 8.1 %collective-permute-start.6 = (bf16[1,2,128,512]{3,1,2,0:T(2,128)(2,1)S(1)}, bf16[1,2,128,512]{3,1,2,0:T(2,128)(2,1)S(1)}, u32[]{:S(2)}, u32[]{:S(2)}) collective-permute-start(bf16[1,2,128,512]{3,1,2,0:T(2,128)(2,1)S(1)} %get-tuple-element.17), channel_id=1, source_target_pairs={{0,1},{1,2},{2,3},{3,4},{4,5},{5,6},{6,7},{8,9},{9,10},{10,11},{11... | collective-permute-start | bytes 786440 | tf_op jit(solution)/shard_map/ppermute | solution.py:12
  98.5 12.8 %collective-permute-start.7 = (bf16[1,2,128,512]{3,1,2,0:T(2,128)(2,1)S(1)}, bf16[1,2,128,512]{3,1,2,0:T(2,128)(2,1)S(1)}, u32[]{:S(2)}, u32[]{:S(2)}) collective-permute-start(bf16[1,2,128,512]{3,1,2,0:T(2,128)(2,1)S(1)} %get-tuple-element.16), channel_id=1, source_target_pairs={{1,0},{2,1},{3,2},{4,3},{5,4},{6,5},{7,6},{9,8},{10,9},{11,10},{12... | collective-permute-start | bytes 786440 | tf_op jit(solution)/shard_map/ppermute | solution.py:15
  112.0 1.2 copy-start.20
  113.2 3.3 copy-start.12
Sparse Core Ops, SparseCore 0:
  27.5 2.3 sort.21.cloned.1.call-done
  (1 shorter events, 0.0 us)
Sparse Core Ops, SparseCore 1:
  69.9 281.2 all-reduce.1
where the time goes:
time: 381 us; the launch traced here: 379 us
  waiting for transfers between devices  242 us (64%)
  local copies, waits for them, and re-layouts  34.2 us (9%)
  other arithmetic  32 us (8%)
  starting transfers between devices  26.2 us (7%)
  matrix products  26.2 us (7%)
  between operations  18.9 us (5%)
    psum x1, waiting for transfers between devices, on_device(): summed = lax.psum(weight_grad, ('gx', 'gy'))  234 us
    ppermute x4, starting transfers between devices, padded(): lax.ppermute(lax.slice_in_dim(block, block.shape[dim] - width, None, axis...  19.5 us
    unnamed x64, local copies, waits for them, and re-layouts  9.38 us
    reduce_sum x3, other arithmetic, on_device(): pieces.append(matrix * lax.rsqrt(jnp.mean(matrix * matrix) + 1e-06))  8.52 us
    ppermute x4, waiting for transfers between devices, padded(): lax.ppermute(lax.slice_in_dim(block, 0, width, axis=dim), axis, backward)  7.98 us
    gather x1, local copies, waits for them, and re-layouts, on_device(): jnp.take_along_axis(grad_s.reshape(tile_count, block_size, feature), inve...  7.83 us
  transfers between devices with their start and end apart: 9, of which 3 were waited for; matrix products, arithmetic and copies ran while one was open for 9% of the time, Pallas kernels for 0%

commit v1 on v0

v1 whole, which is shorter than its diff:
```python
import functools

import jax
import jax.numpy as jnp
from jax import lax
from jax.experimental import pallas as pl
from jax.experimental.pallas import tpu as pltpu
from jax.sharding import PartitionSpec as P

MESH = pl.DeviceIdType.MESH
F32 = jnp.float32
BF16 = jnp.bfloat16
D = 512
H = 256
Q = 128
ROWS = 7 * D
CHIP_ROWS = 28
BLK = 112
NGROUP = 8
EARLY = 5
BOUNDS = (3 * D, 4 * D, 6 * D)
SIZES = (3 * D * D, D * D, 2 * D * D, D * D)
PIECES = ((4 * D, 3 * D), (3 * D, D), (0, D), (D, D), (2 * D, D))


def dot(a, b):
    return jnp.dot(a, b, preferred_element_type=F32)


def dot_t(a, b):
    return lax.dot_general(a, b, (((1,), (1,)), ((), ())), preferred_element_type=F32)


def t_dot(a, b):
    return lax.dot_general(a, b, (((0,), (0,)), ((), ())), preferred_element_type=F32)


def normed_rows(values):
    center = values - jnp.mean(values, axis=-1, keepdims=True)
    inv = lax.rsqrt(jnp.mean(center * center, axis=-1, keepdims=True) + 1e-05)
    return center * inv, inv


def norm_back(normed, inv, up):
    return inv * (
        up
        - jnp.mean(up, axis=-1, keepdims=True)
        - normed * jnp.mean(up * normed, axis=-1, keepdims=True)
    )


def silu_parts(v):
    s = jax.nn.sigmoid(v)
    return (v * s).astype(BF16), s * (1.0 + v * (1.0 - s))


def picked(flag):
    return jnp.where(flag, 1.0, 0.0).astype(F32)


def kernel(
    count_s, list_s, recv_s, send_s, perm_ref, eb1, nb1,
    nodes_h, edges_h, ew1_h, ew2_h, nw1_h, nw2_h, cotn_h, cote_h,
    nout_h, ngrad_h, egrad_h, wdir,
    loc, ext, edges, ew1, ew2, nw1, nw2, cotn, cote, pack, pt, pm,
    hr, hs, aff, hid, msg, einv, agg, gagg, owned, gea, geap, gel_p,
    nin, gna_p, gnl_p, xs, hret, ret, nout, ngrad, egrad,
    gsend, gown, grecv, g1a, g1b, r1a, r1b, g2a, g2b, r2a, r2b,
    g3, s3, r3, fin, swap_s, swap_r, stat_s, stat_r, flat,
    in_sem, out_sem, hs_sem, hr_sem, bs_sem, br_sem, cs_sem, cr_sem,
    as_sem, ar_sem, ys_sem, yr_sem, a2s_sem, a2r_sem, b2s_sem, b2r_sem,
    zs_sem, zr_sem, ws_sem, wr_sem, ts_sem, tr_sem,
):
    gx = lax.axis_index("gx")
    gy = lax.axis_index("gy")
    y = gx // 8
    z_lo = (gx // 4) % 2
    x = gx % 4
    z_hi = gy // 2
    core = gy % 2
    z = z_hi * 2 + z_lo
    other = (gx, z_hi * 2 + (1 - core))

    def x_peer(k):
        to = (x + k) % 4
        return to, (y * 8 + z_lo * 4 + to, gy)

    def y_peer(k):
        to = (y + k) % 4
        return to, (to * 8 + z_lo * 4 + x, gy)

    def z_peer(k):
        to = (z + k) % 8
        lo, hi = to % 2, to // 2
        return lo * 4 + hi, (y * 8 + lo * 4 + x, hi * 2 + core)

    nxt = ((gx + 1, gy), (gx - 1, gy), (gx, gy + 1), (gx, gy - 1))
    has = (gx < 31, gx > 0, gy < 7, gy > 0)

    loads = [
        pltpu.make_async_copy(src, dst, in_sem.at[i])
        for i, (src, dst) in enumerate(
            (
                (nodes_h, loc),
                (edges_h, edges),
                (ew1_h, ew1),
                (ew2_h, ew2),
                (nw1_h, nw1),
                (nw2_h, nw2),
                (cotn_h, cotn),
                (cote_h, cote),
                (nodes_h, ext.at[pl.ds(0, 2)]),
            )
        )
    ]
    for load in loads:
        load.start()

    barrier = pltpu.get_barrier_semaphore()
    fixed = [other]
    fixed += [x_peer(k)[1] for k in range(1, 4)]
    fixed += [y_peer(k)[1] for k in range(1, 4)]
    fixed += [z_peer(k)[1] for k in range(1, 8)]
    for q in range(4):

        @pl.when(has[q])
        def _():
            pl.semaphore_signal(barrier, inc=1, device_id=nxt[q], device_id_type=MESH)

    for peer in fixed:
        pl.semaphore_signal(barrier, inc=1, device_id=peer, device_id_type=MESH)

    loads[0].wait()
    for q in range(4):
        for s in range(2):
            pack[q, s] = loc[list_s[0, 0, q, s]]

    peers = len(fixed)
    for flag in has:
        peers += jnp.where(flag, 1, 0)
    pl.semaphore_wait(barrier, peers)

    def remote(src, dst, send, recv, to):
        return pltpu.make_async_remote_copy(
            src_ref=src, dst_ref=dst, send_sem=send, recv_sem=recv,
            device_id=to, device_id_type=MESH,
        )

    halo = [
        remote(pack.at[q], ext.at[pl.ds(2 + 2 * q, 2)], hs_sem.at[q], hr_sem.at[q], nxt[q])
        for q in range(4)
    ]
    for q in range(4):

        @pl.when(has[q])
        def _():
            halo[q].start()

    loads[1].wait()
    loads[2].wait()
    lane = lax.broadcasted_iota(jnp.int32, (Q, Q), 0)

    def before(i, c):
        rows = pl.ds(i * H, H)
        for u in range(2):
            t = 2 * i + u
            hot = picked(lane == perm_ref[0, 0, pl.ds(t, 1), :])
            pt[t] = hot.astype(BF16)
            pm[t] = hot.T.astype(BF16)
            hr[pl.ds(t * Q, Q), :] = loc[recv_s[0, 0, t]]
        aff[rows, :] = (
            dot(edges[rows, :], ew1[pl.ds(0, D), :])
            + dot(hr[rows, :], ew1[pl.ds(D, D), :])
            + eb1[...]
        )
        return c

    for q in range(4):

        @pl.when(has[q])
        def _():
            halo[q].wait_send()

    lax.fori_loop(0, 3, before, 0)
    agg[...] = jnp.zeros_like(agg)
    for load in loads[3:]:
        load.wait()
    came = (gx > 0, gx < 31, gy > 0, gy < 7)
    for q in range(4):

        @pl.when(came[q])
        def _():
            halo[q].wait_recv()

    def forward(i, c):
        rows = pl.ds(i * H, H)
        for u in range(2):
            t = 2 * i + u
            hs[pl.ds(t * Q, Q), :] = dot(pm[t], ext[send_s[0, 0, t]]).astype(BF16)
        hidden, slope = silu_parts(aff[rows, :] + dot(hs[rows, :], ew1[pl.ds(2 * D, D), :]))
        hid[rows, :] = hidden
        aff[rows, :] = slope
        message, inv = normed_rows(dot(hidden, ew2[...]))
        msg[rows, :] = message
        einv[rows, :] = inv
        for b in range(2):
            agg[b] += message[:Q] * picked(recv_s[0, 0, 2 * i] == b) + message[Q:] * picked(
                recv_s[0, 0, 2 * i + 1] == b
            )
        return c

    lax.fori_loop(0, 3, forward, 0)

    mine_cols = pl.ds(pl.multiple_of(core * H, H), H)
    their_cols = pl.ds(pl.multiple_of((1 - core) * H, H), H)
    for b in range(2):
        nin[pl.ds(b * Q, Q), pl.ds(0, D)] = loc[b]
        nin[pl.ds(b * Q, Q), pl.ds(D, D)] = agg[b].astype(BF16)
    nhid, nslope = silu_parts(dot(nin[...], nw1[...]) + nb1[...])
    nmsg, ninv = normed_rows(dot(nhid, nw2[...]))
    nout[...] = (nin[:, :D].astype(F32) + nmsg).astype(BF16)
    out_node = pltpu.make_async_copy(nout, nout_h, out_sem.at[0])
    out_node.start()
    gnl = norm_back(nmsg, ninv, cotn[...].astype(F32)).astype(BF16)
    gel_p[pl.ds(0, H), :] = gnl
    gnl_p[:, pl.ds(0, H)] = gel_p[pl.ds(0, H), their_cols]
    gnl_p[:, pl.ds(H, H)] = gel_p[pl.ds(0, H), mine_cols]
    gna = (dot_t(gnl, nw2[...]) * nslope).astype(BF16)
    gel_p[pl.ds(0, H), :] = gna
    gna_p[:, pl.ds(0, H)] = gel_p[pl.ds(0, H), their_cols]
    gna_p[:, pl.ds(H, H)] = gel_p[pl.ds(0, H), mine_cols]
    ginput = dot_t(gna, nw1[...])
    for b in range(2):
        owned[b] = ginput[b * Q : (b + 1) * Q, :D]
        gagg[b] = ginput[b * Q : (b + 1) * Q, D:]

    cores = [
        remote(
            gsend.at[pl.ds(lo, n), :], grecv.at[pl.ds(lo, n), :],
            cs_sem.at[i], cr_sem.at[i], other,
        )
        for i, (lo, n) in enumerate(PIECES)
    ]

    def put(at, value):
        gsend[pl.ds(at, H), :] = value[:, :H].astype(BF16)
        gown[pl.ds(at, H), :] = value[:, H:]

    def outer(left, right, base, blocks):
        def one(j, c):
            j = pl.multiple_of(j * H, H)
            put(base + j, t_dot(left[:, pl.ds(j, H)], right[...]))
            return c

        lax.fori_loop(0, blocks, one, 0)

    geap[pl.ds(0, H), :] = nhid
    outer_rows = geap.at[pl.ds(0, H), :]
    outer(outer_rows, gnl_p, 6 * D, 2)
    outer(nin, gna_p, 4 * D, 4)
    cores[0].start()

    def backward(i, c):
        rows = pl.ds(i * H, H)
        up = jnp.concatenate(
            [gagg[recv_s[0, 0, 2 * i]], gagg[recv_s[0, 0, 2 * i + 1]]], axis=0
        ) + cote[rows, :].astype(F32)
        gel = norm_back(msg[rows, :], einv[rows, :], up).astype(BF16)
        gea[rows, :] = gel
        gel_p[rows, pl.ds(0, H)] = gea[rows, their_cols]
        gel_p[rows, pl.ds(H, H)] = gea[rows, mine_cols]
        gea[rows, :] = (dot_t(gel, ew2[...]) * aff[rows, :]).astype(BF16)
        geap[rows, pl.ds(0, H)] = gea[rows, their_cols]
        geap[rows, pl.ds(H, H)] = gea[rows, mine_cols]
        return c

    lax.fori_loop(0, 3, backward, 0)
    outer(hid, gel_p, 3 * D, 2)
    cores[1].start()

    def pair_sum(lo, hi):
        def one(j, c):
            rows = pl.ds(pl.multiple_of(j * BLK, 16), BLK)
            total = (gown[rows, :] + grecv[rows, :].astype(F32)).astype(BF16)
            g1a[j // 4, j % 4] = total[:, :Q]
            g1b[j // 4, j % 4] = total[:, Q:]
            return c

        lax.fori_loop(lo, hi, one, 0)

    early, late, sides = [], [], []
    for k in range(1, 4):
        to, who = x_peer(k)
        for got, lo, n, sem in ((early, EARLY, NGROUP - EARLY, 0), (late, 0, EARLY, 3)):
            got.append(
                remote(
                    g1a.at[pl.ds(lo, n), to], r1a.at[k - 1, pl.ds(lo, n)],
                    as_sem.at[sem + k - 1], ar_sem.at[sem + k - 1], who,
                )
            )
        to, who = y_peer(k)
        sides.append(
            remote(
                g1b.at[pl.ds(2 * to, 2)], r1b.at[k - 1],
                ys_sem.at[k - 1], yr_sem.at[k - 1], who,
            )
        )

    cores[0].wait_recv()
    pair_sum(4 * EARLY, 32)
    for copy in early:
        copy.start()

    outer(edges, geap, 0, 2)
    cores[2].start()
    outer(hr, geap, D, 2)
    cores[3].start()
    outer(hs, geap, 2 * D, 2)
    cores[4].start()
    for copy in cores[1:]:
        copy.wait_recv()
    pair_sum(0, 4 * EARLY)
    for copy in sides:
        copy.start()
    for copy in late:
        copy.start()

    def inputs(i, c):
        rows = pl.ds(i * H, H)
        part = gea[rows, :]
        egrad[rows, :] = (
            cote[rows, :].astype(F32) + dot_t(part, ew1[pl.ds(0, D), :])
        ).astype(BF16)
        grad_r = dot_t(part, ew1[pl.ds(D, D), :])
        for b in range(2):
            owned[b] += grad_r[:Q] * picked(recv_s[0, 0, 2 * i] == b) + grad_r[Q:] * picked(
                recv_s[0, 0, 2 * i + 1] == b
            )
        for u in range(2):
            t = 2 * i + u
            rows_t = pl.ds(t * Q, Q)
            hs[rows_t, :] = dot(pt[t], gea[rows_t, :]).astype(BF16)
        grad_s = dot_t(hs[rows, :], ew1[pl.ds(2 * D, D), :])
        for u in range(2):
            xs[2 * i + u] = grad_s[u * Q : (u + 1) * Q]
        return c

    lax.fori_loop(0, 3, inputs, 0)
    out_edge = pltpu.make_async_copy(egrad, egrad_h, out_sem.at[1])
    out_edge.start()

    def slots(b, c):
        total = xs[0] * picked(send_s[0, 0, 0] == b + 2)
        for t in range(1, 6):
            total += xs[t] * picked(send_s[0, 0, t] == b + 2)
        hret[b // 2, b % 2] = total.astype(BF16)
        return c

    lax.fori_loop(0, 8, slots, 0)
    back = (nxt[1], nxt[0], nxt[3], nxt[2])
    home = [
        remote(hret.at[q], ret.at[q], bs_sem.at[q], br_sem.at[q], back[q]) for q in range(4)
    ]
    for q in range(4):

        @pl.when(came[q])
        def _():
            home[q].start()

    for b in range(2):
        total = owned[b] + cotn[pl.ds(b * Q, Q), :].astype(F32)
        for t in range(6):
            total += xs[t] * picked(send_s[0, 0, t] == b)
        owned[b] = total

    for copy in early + late:
        copy.wait_recv()

    def sum_a(g, c):
        total = g1a[g, x].astype(F32)
        for k in range(3):
            total += r1a[k, g].astype(F32)
        g2a[g // 2, g % 2] = total.astype(BF16)
        return c

    lax.fori_loop(0, NGROUP, sum_a, 0)
    second_a, second_b = [], []
    for k in range(1, 4):
        to, who = y_peer(k)
        second_a.append(
            remote(g2a.at[to], r2a.at[k - 1], a2s_sem.at[k - 1], a2r_sem.at[k - 1], who)
        )
        to, who = x_peer(k)
        second_b.append(
            remote(g2b.at[to], r2b.at[k - 1], b2s_sem.at[k - 1], b2r_sem.at[k - 1], who)
        )
    for copy in second_a:
        copy.start()
    for copy in sides:
        copy.wait_recv()

    def sum_b(j, c):
        total = g1b[2 * y + j // 4, j % 4].astype(F32)
        for k in range(3):
            total += r1b[k, j // 4, j % 4].astype(F32)
        g2b[j % 4, j // 4] = total.astype(BF16)
        return c

    lax.fori_loop(0, NGROUP, sum_b, 0)
    for copy in second_b:
        copy.start()

    for copy in second_a + second_b:
        copy.wait_recv()
    for g in range(2):
        total = g2a[y, g].astype(F32)
        for k in range(3):
            total += r2a[k, g].astype(F32)
        g3[g, pl.ds(0, BLK), pl.ds(0, Q)] = total
        total = g2b[x, g].astype(F32)
        for k in range(3):
            total += r2b[k, g].astype(F32)
        g3[g, pl.ds(0, BLK), pl.ds(Q, Q)] = total
        g3[g, pl.ds(BLK, 16), :] = jnp.zeros((16, H), F32)
        for h in range(4):
            s3[4 * g + h] = g3[g, pl.ds(CHIP_ROWS * h, 32), :].astype(BF16)
    along = []
    for k in range(1, 8):
        to, who = z_peer(k)
        along.append(
            remote(s3.at[to], r3.at[k - 1], zs_sem.at[k - 1], zr_sem.at[k - 1], who)
        )
    for copy in along:
        copy.start()

    has_home = has
    for q in range(4):

        @pl.when(has_home[q])
        def _():
            home[q].wait_recv()

    for b in range(2):
        total = owned[b]
        for q in range(4):
            for s in range(2):
                wanted = jnp.logical_and(list_s[0, 0, q, s] == b, count_s[0, 0, q] > s)
                weight = jnp.where(wanted, 1, 0) * jnp.ones((Q, D), jnp.int32)
                total += jnp.where(weight > 0, ret[q, s].astype(F32), 0.0)
        ngrad[pl.ds(b * Q, Q), :] = total.astype(BF16)
    out_grad = pltpu.make_async_copy(ngrad, ngrad_h, out_sem.at[2])
    out_grad.start()

    for copy in along:
        copy.wait_recv()
    total = s3[z_lo * 4 + z_hi].astype(F32)
    for k in range(7):
        total += r3[k].astype(F32)
    fin[...] = total

    first = fin[pl.ds(0, 16), :]
    second = fin[pl.ds(14, 16), :]
    swap_s[...] = jnp.where(core == 0, second, first)
    swap = remote(swap_s, swap_r, ws_sem, wr_sem, other)
    swap.start()

    local = lax.broadcasted_iota(jnp.int32, (32, H), 0)
    row = local + CHIP_ROWS * (gx * 4 + z_hi)
    square = jnp.where(local < CHIP_ROWS, total * total, 0.0)
    square = square[:, :Q] + square[:, Q:]
    row = row[:, :Q]
    cuts = (0,) + BOUNDS + (ROWS,)
    pieces = [
        jnp.sum(
            jnp.where(jnp.logical_and(row >= cuts[m], row < cuts[m + 1]), square, 0.0),
            axis=0, keepdims=True,
        )
        for m in range(4)
    ]
    stat = jnp.concatenate(pieces + [jnp.zeros((4, Q), F32)], axis=0)
    rounds = (
        [other],
        [z_peer(k)[1] for k in range(1, 8)],
        [x_peer(k)[1] for k in range(1, 4)],
        [y_peer(k)[1] for k in range(1, 4)],
    )
    at = 0
    stat_copies = []
    for r, peers in enumerate(rounds):
        stat_s[r] = stat
        now = [
            remote(stat_s.at[r], stat_r.at[at + i], ts_sem.at[at + i], tr_sem.at[at + i], who)
            for i, who in enumerate(peers)
        ]
        for copy in now:
            copy.start()
        for copy in now:
            copy.wait_recv()
        for i in range(len(peers)):
            stat = stat + stat_r[at + i]
        at += len(peers)
        stat_copies += now

    swap.wait_recv()
    keep = jnp.where(core == 0, first, second)
    scales = [
        lax.rsqrt(jnp.sum(stat[m : m + 1], axis=-1, keepdims=True) * (1.0 / SIZES[m]) + 1e-06)
        for m in range(4)
    ]
    row = lax.broadcasted_iota(jnp.int32, (16, H), 0) + 14 * (gx * 8 + gy)
    scale = jnp.where(
        row < BOUNDS[0],
        scales[0],
        jnp.where(row < BOUNDS[1], scales[1], jnp.where(row < BOUNDS[2], scales[2], scales[3])),
    )
    theirs = swap_r[...]
    left = jnp.where(core == 0, keep, theirs) * scale
    right = jnp.where(core == 0, theirs, keep) * scale
    for g in range(2):
        flat[pl.ds(g, 16, stride=4), :] = left[:, g * Q : (g + 1) * Q]
        flat[pl.ds(2 + g, 16, stride=4), :] = right[:, g * Q : (g + 1) * Q]
    wdir[...] = flat[pl.ds(0, 56), :].astype(BF16)

    for q in range(4):

        @pl.when(came[q])
        def _():
            home[q].wait_send()

    for copy in cores + early + late + sides + second_a + second_b + along + stat_copies:
        copy.wait_send()
    swap.wait_send()
    out_node.wait()
    out_edge.wait()
    out_grad.wait()


def on_device(
    node_latents, edge_latents, edge_w1, edge_b1, edge_w2, node_w1, node_b1, node_w2,
    node_cot, edge_cot, send_count, send_list, tile_recv, tile_send, tile_perm,
):
    hbm = pl.BlockSpec(memory_space=pl.ANY)
    vmem = pl.BlockSpec(memory_space=pltpu.VMEM)
    smem = pl.BlockSpec(memory_space=pltpu.SMEM)
    b = functools.partial(pltpu.VMEM, dtype=BF16)
    f = functools.partial(pltpu.VMEM, dtype=F32)
    sem = lambda n: pltpu.SemaphoreType.DMA((n,))
    one = pltpu.SemaphoreType.DMA
    scratch = [
        b((2, Q, D)), b((10, Q, D)), b((768, D)), b((3 * D, D)), b((D, D)), b((2 * D, D)), b((D, D)),
        b((H, D)), b((768, D)), b((4, 2, Q, D)), b((6, Q, Q)), b((6, Q, Q)),
        b((768, D)), b((768, D)), f((768, D)), b((768, D)), f((768, D)), f((768, 1)),
        f((2, Q, D)), f((2, Q, D)), f((2, Q, D)), b((768, D)), b((768, D)), b((768, D)),
        b((H, 2 * D)), b((H, D)), b((H, D)), f((6, Q, D)), b((4, 2, Q, D)), b((4, 2, Q, D)),
        b((H, D)), b((H, D)), b((768, D)),
        b((ROWS, H)), f((ROWS, H)), b((ROWS, H)),
        b((8, 4, BLK, Q)), b((8, 4, BLK, Q)), b((3, 8, BLK, Q)), b((3, 2, 4, BLK, Q)),
        b((4, 2, BLK, Q)), b((4, 2, BLK, Q)), b((3, 2, BLK, Q)), b((3, 2, BLK, Q)),
        f((2, Q, H)), b((8, 32, H)), b((7, 32, H)), f((32, H)), f((16, H)), f((16, H)),
        f((4, 8, Q)), f((14, 8, Q)), f((64, Q)),
        sem(9), sem(3), sem(4), sem(4), sem(4), sem(4), sem(5), sem(5),
        sem(6), sem(6), sem(3), sem(3), sem(3), sem(3), sem(3), sem(3),
        sem(7), sem(7), one, one, sem(14), sem(14),
    ]
    nout, ngrad, egrad, wdir = pl.pallas_call(
        kernel,
        out_shape=(
            jax.ShapeDtypeStruct((H, D), BF16),
            jax.ShapeDtypeStruct((H, D), BF16),
            jax.ShapeDtypeStruct((768, D), BF16),
            jax.ShapeDtypeStruct((56, Q), BF16),
        ),
        in_specs=[smem] * 4 + [vmem] * 3 + [hbm] * 8,
        out_specs=(hbm, hbm, hbm, vmem),
        scratch_shapes=scratch,
        compiler_params=pltpu.CompilerParams(
            collective_id=0, has_side_effects=True, vmem_limit_bytes=56 * 1024 * 1024
        ),
        name="layer",
    )(
        send_count, send_list, tile_recv, tile_send, tile_perm,
        edge_b1.reshape(1, D), node_b1.reshape(1, D),
        node_latents.reshape(2, Q, D), edge_latents.reshape(768, D),
        edge_w1, edge_w2, node_w1, node_w2,
        node_cot.reshape(H, D), edge_cot.reshape(768, D),
    )
    return (
        nout.reshape(1, 1, H, D),
        ngrad.reshape(1, 1, H, D),
        egrad.reshape(1, 1, 768, D),
        wdir.reshape(7168),
    )


def solution(mesh):
    cells = P("gx", "gy", None, None)
    flat = P("gx", "gy", None)
    return jax.shard_map(
        on_device,
        mesh=mesh,
        in_specs=(
            cells, cells, P(), P(), P(), P(), P(), P(), cells, cells,
            flat, cells, flat, flat, cells,
        ),
        out_specs=(cells, cells, cells, P(("gx", "gy"))),
        check_vma=False,
    )
```

time: 381 us -> 84.7 us (0.22)
  waiting for transfers between devices: 242 us -> 0 us
  Pallas kernels: 0 us -> 76.3 us
  other arithmetic: 32 us -> 0 us
  local copies, waits for them, and re-layouts: 34.2 us -> 7.51 us
  matrix products: 26.2 us -> 0 us
  starting transfers between devices: 26.2 us -> 0 us
  between operations: 18.9 us -> 0.66 us
    psum x1 -> x0, waiting for transfers between devices: 234 us -> none  [on_device(): summed = lax.psum(weight_grad, ('gx', 'gy'))]
    pallas_call x0 -> x1, Pallas kernels: none -> 76.3 us  [on_device(): pl.pallas_call(kernel, out_shape=(jax.ShapeDtypeStruct((H, D), BF16), jax...]
    dot_general x16 -> x0, matrix products: 26.2 us -> none  [the longest x4 5.82 us: matmul(): return jnp.dot(factor, second, preferred_element_type=jnp.float32)]
    ppermute x8 -> x0, starting transfers between devices: 26.1 us -> none  [the longest x4 19.5 us: padded(): lax.ppermute(lax.slice_in_dim(block, block.shape[dim] - width, None, axis...]
    gather x5 -> x0, local copies, waits for them, and re-layouts: 19.2 us -> none  [the longest x1 7.83 us: on_device(): jnp.take_along_axis(grad_s.reshape(tile_count, block_size, feature), inve...]
    reduce_sum x8 -> x0, other arithmetic: 12.8 us -> none  [the longest x3 8.52 us: on_device(): pieces.append(matrix * lax.rsqrt(jnp.mean(matrix * matrix) + 1e-06))]
    ppermute x8 -> x0, waiting for transfers between devices: 7.99 us -> none  [the longest x4 7.98 us: padded(): lax.ppermute(lax.slice_in_dim(block, 0, width, axis=dim), axis, backward)]
    mul x6 -> x0, other arithmetic: 6.26 us -> none  [the longest x3 5.99 us: on_device(): pieces.append(matrix * lax.rsqrt(jnp.mean(matrix * matrix) + 1e-06))]
  transfers between devices with their start and end apart: 9 -> 0, of which waited for: 3 -> 0; matrix products, arithmetic and copies ran while one was open for 9% -> 0% of each run, Pallas kernels for 0% -> 0%
where the time goes in v1:
time: 84.7 us; the launch traced here: 84.5 us
  Pallas kernels  76.3 us (90%)
  local copies, waits for them, and re-layouts  7.51 us (9%)
    pallas_call x1, Pallas kernels, on_device(): pl.pallas_call(kernel, out_shape=(jax.ShapeDtypeStruct((H, D), BF16), jax...  76.3 us
    unnamed x10, local copies, waits for them, and re-layouts  7.51 us

profile of v1, /device:TPU:1, one launch (start us, length us, event | category | flops | bytes accessed | tf_op | source)
XLA Modules:
  0.0 84.5 jit_solution(5441551321289075868)
XLA Ops:
  0.6 1.3 %copy.19.list_s = s32[1,1,4,2]{3,2,1,0:T(4,128)} copy(s32[1,1,4,2]{2,3,1,0:T(2,128)} %param.26) | data formatting | bytes 64 | tf_op args[11]
  2.0 1.3 %copy.20.perm_ref = s32[1,1,6,128]{3,2,1,0:T(8,128)} copy(s32[1,1,6,128]{3,1,2,0:T(1,128)} %param.29) | data formatting | bytes 6144 | tf_op args[14]
  3.2 76.3 %layer.1 = (bf16[256,512]{1,0:T(8,128)(2,1)}, bf16[256,512]{1,0:T(8,128)(2,1)}, bf16[768,512]{1,0:T(8,128)(2,1)}, bf16[56,128]{1,0:T(8,128)(2,1)}) custom-call(s32[1,1,4]{2,1,0:T(1,128)} %count_s.1, s32[1,1,4,2]{3,2,1,0:T(4,128)} %copy.19.list_s, s32[1,1,6]{2,1,0:T(1,128)} %recv_s.1, s32[1,1,6]{2,1,0:T(1,128)} %send_s.1, s32[1,1,6,128]{3,2,1,0:T(8,128)} %copy.20.perm_ref, ...), custom_call_target="tpu_custom_call" | custom-call | tf_op jit(solution)/shard_map/layer/pallas_call | solution.py:565
  79.6 0.0 copy-start
  79.6 0.0 copy-start.1
  79.6 1.7 %copy.25 = bf16[1,1,256,512]{3,2,1,0:T(8,128)(2,1)} copy(bf16[1,1,256,512]{3,2,1,0:T(8,128)(2,1)} %bitcast.16) | data formatting | bytes 524288
  81.4 1.7 %copy.26 = bf16[1,1,256,512]{3,2,1,0:T(8,128)(2,1)} copy(bf16[1,1,256,512]{3,2,1,0:T(8,128)(2,1)} %bitcast.15) | data formatting | bytes 524288
  83.0 0.0 copy-done
  83.0 0.9 %copy.27 = bf16[1,1,768,512]{3,2,1,0:T(8,128)(2,1)} copy(bf16[1,1,768,512]{3,2,1,0:T(8,128)(2,1)S(1)} %bitcast.12) | data formatting | bytes 1572864
  83.9 0.0 copy-done.1
  83.9 0.6 copy.28
Async XLA Ops:
  79.6 3.4 %copy-start = (bf16[768,512]{1,0:T(8,128)(2,1)S(1)}, bf16[768,512]{1,0:T(8,128)(2,1)}, u32[]{:S(2)}) copy-start(bf16[768,512]{1,0:T(8,128)(2,1)} %get-tuple-element.10) | copy-start | bytes 2359300
  79.6 4.3 %copy-start.1 = (bf16[56,128]{1,0:T(8,128)(2,1)S(1)}, bf16[56,128]{1,0:T(8,128)(2,1)}, u32[]{:S(2)}) copy-start(bf16[56,128]{1,0:T(8,128)(2,1)} %get-tuple-element.11) | copy-start | bytes 43012

commit v2 on v1

--- a/solution.py
+++ b/solution.py
@@ -94,6 +94,9 @@
         lo, hi = to % 2, to // 2
         return lo * 4 + hi, (y * 8 + lo * 4 + x, hi * 2 + core)
 
+    own_blk = z_lo * 16 + ((y + 4 - x) % 4) * 4 + x
+    from_gx = ((gx // 4 + x) % 4) * 8 + (gx // 16) * 4 + x
+
     nxt = ((gx + 1, gy), (gx - 1, gy), (gx, gy + 1), (gx, gy - 1))
     has = (gx < 31, gx > 0, gy < 7, gy > 0)
 
@@ -133,7 +136,7 @@
     loads[0].wait()
     for q in range(4):
         for s in range(2):
-            pack[q, s] = loc[list_s[0, 0, q, s]]
+            pack[q, s] = loc[list_s[0, 0, s, q]]
 
     peers = len(fixed)
     for flag in has:
@@ -164,7 +167,7 @@
         rows = pl.ds(i * H, H)
         for u in range(2):
             t = 2 * i + u
-            hot = picked(lane == perm_ref[0, 0, pl.ds(t, 1), :])
+            hot = picked(lane == perm_ref[0, t])
             pt[t] = hot.astype(BF16)
             pm[t] = hot.T.astype(BF16)
             hr[pl.ds(t * Q, Q), :] = loc[recv_s[0, 0, t]]
@@ -283,28 +286,28 @@
             rows = pl.ds(pl.multiple_of(j * BLK, 16), BLK)
             total = (gown[rows, :] + grecv[rows, :].astype(F32)).astype(BF16)
             g1a[j // 4, j % 4] = total[:, :Q]
-            g1b[j // 4, j % 4] = total[:, Q:]
+            g1b[j // 4, (j // 4 + j) % 4] = total[:, Q:]
             return c
 
         lax.fori_loop(lo, hi, one, 0)
 
-    early, late, sides = [], [], []
-    for k in range(1, 4):
-        to, who = x_peer(k)
-        for got, lo, n, sem in ((early, EARLY, NGROUP - EARLY, 0), (late, 0, EARLY, 3)):
+    early, late = [], []
+    for got, lo, n, sem in ((early, EARLY, NGROUP - EARLY, 0), (late, 0, EARLY, 3)):
+        for k in range(1, 4):
+            to, who = x_peer(k)
             got.append(
                 remote(
                     g1a.at[pl.ds(lo, n), to], r1a.at[k - 1, pl.ds(lo, n)],
                     as_sem.at[sem + k - 1], ar_sem.at[sem + k - 1], who,
                 )
             )
-        to, who = y_peer(k)
-        sides.append(
-            remote(
-                g1b.at[pl.ds(2 * to, 2)], r1b.at[k - 1],
-                ys_sem.at[k - 1], yr_sem.at[k - 1], who,
+            to, who = y_peer(k)
+            got.append(
+                remote(
+                    g1b.at[pl.ds(lo, n), to], r1b.at[k - 1, pl.ds(lo, n)],
+                    ys_sem.at[sem + k - 1], yr_sem.at[sem + k - 1], who,
+                )
             )
-        )
 
     cores[0].wait_recv()
     pair_sum(4 * EARLY, 32)
@@ -320,8 +323,6 @@
     for copy in cores[1:]:
         copy.wait_recv()
     pair_sum(0, 4 * EARLY)
-    for copy in sides:
-        copy.start()
     for copy in late:
         copy.start()
 
@@ -373,44 +374,37 @@
             total += xs[t] * picked(send_s[0, 0, t] == b)
         owned[b] = total
 
-    for copy in early + late:
-        copy.wait_recv()
-
-    def sum_a(g, c):
+    def sum_first(g, c):
         total = g1a[g, x].astype(F32)
         for k in range(3):
             total += r1a[k, g].astype(F32)
-        g2a[g // 2, g % 2] = total.astype(BF16)
+        g2a[(g + x) % 4, g // 4] = total.astype(BF16)
+        total = g1b[g, y].astype(F32)
+        for k in range(3):
+            total += r1b[k, g].astype(F32)
+        g2b[(y + 8 - g) % 4, g // 4] = total.astype(BF16)
         return c
 
-    lax.fori_loop(0, NGROUP, sum_a, 0)
-    second_a, second_b = [], []
+    for copy in early:
+        copy.wait_recv()
+    lax.fori_loop(EARLY, NGROUP, sum_first, 0)
+    for copy in late:
+        copy.wait_recv()
+    lax.fori_loop(0, EARLY, sum_first, 0)
+    second = []
     for k in range(1, 4):
         to, who = y_peer(k)
-        second_a.append(
+        second.append(
             remote(g2a.at[to], r2a.at[k - 1], a2s_sem.at[k - 1], a2r_sem.at[k - 1], who)
         )
         to, who = x_peer(k)
-        second_b.append(
+        second.append(
             remote(g2b.at[to], r2b.at[k - 1], b2s_sem.at[k - 1], b2r_sem.at[k - 1], who)
         )
-    for copy in second_a:
+    for copy in second:
         copy.start()
-    for copy in sides:
-        copy.wait_recv()
-
-    def sum_b(j, c):
-        total = g1b[2 * y + j // 4, j % 4].astype(F32)
-        for k in range(3):
-            total += r1b[k, j // 4, j % 4].astype(F32)
-        g2b[j % 4, j // 4] = total.astype(BF16)
-        return c
-
-    lax.fori_loop(0, NGROUP, sum_b, 0)
-    for copy in second_b:
-        copy.start()
-
-    for copy in second_a + second_b:
+
+    for copy in second:
         copy.wait_recv()
     for g in range(2):
         total = g2a[y, g].astype(F32)
@@ -433,24 +427,6 @@
     for copy in along:
         copy.start()
 
-    has_home = has
-    for q in range(4):
-
-        @pl.when(has_home[q])
-        def _():
-            home[q].wait_recv()
-
-    for b in range(2):
-        total = owned[b]
-        for q in range(4):
-            for s in range(2):
-                wanted = jnp.logical_and(list_s[0, 0, q, s] == b, count_s[0, 0, q] > s)
-                weight = jnp.where(wanted, 1, 0) * jnp.ones((Q, D), jnp.int32)
-                total += jnp.where(weight > 0, ret[q, s].astype(F32), 0.0)
-        ngrad[pl.ds(b * Q, Q), :] = total.astype(BF16)
-    out_grad = pltpu.make_async_copy(ngrad, ngrad_h, out_sem.at[2])
-    out_grad.start()
-
     for copy in along:
         copy.wait_recv()
     total = s3[z_lo * 4 + z_hi].astype(F32)
@@ -458,14 +434,44 @@
         total += r3[k].astype(F32)
     fin[...] = total
 
-    first = fin[pl.ds(0, 16), :]
-    second = fin[pl.ds(14, 16), :]
-    swap_s[...] = jnp.where(core == 0, second, first)
-    swap = remote(swap_s, swap_r, ws_sem, wr_sem, other)
-    swap.start()
+    def node_gradient():
+        for q in range(4):
+
+            @pl.when(has[q])
+            def _():
+                home[q].wait_recv()
+
+        for b in range(2):
+            total = owned[b]
+            for q in range(4):
+                for s in range(2):
+                    wanted = jnp.logical_and(list_s[0, 0, s, q] == b, count_s[0, 0, q] > s)
+                    weight = jnp.where(wanted, 1, 0) * jnp.ones((Q, D), jnp.int32)
+                    total += jnp.where(weight > 0, ret[q, s].astype(F32), 0.0)
+            ngrad[pl.ds(b * Q, Q), :] = total.astype(BF16)
+        out_grad = pltpu.make_async_copy(ngrad, ngrad_h, out_sem.at[2])
+        out_grad.start()
+        return out_grad
+
+    swap_s[0] = fin[pl.ds(0, 16), :]
+    swap_s[1] = fin[pl.ds(14, 16), :]
+    swap = [
+        remote(swap_s.at[c], swap_r.at[core], ws_sem.at[c], wr_sem.at[core], (own_blk, z_hi * 2 + c))
+        for c in range(2)
+    ]
+    stay = pltpu.make_async_copy(swap_s.at[core], swap_r.at[core], in_sem.at[0])
+    for c in range(2):
+
+        @pl.when(jnp.logical_or(own_blk != gx, core != c))
+        def _():
+            swap[c].start()
+
+    @pl.when(own_blk == gx)
+    def _():
+        stay.start()
 
     local = lax.broadcasted_iota(jnp.int32, (32, H), 0)
-    row = local + CHIP_ROWS * (gx * 4 + z_hi)
+    row = local + CHIP_ROWS * (own_blk * 4 + z_hi)
     square = jnp.where(local < CHIP_ROWS, total * total, 0.0)
     square = square[:, :Q] + square[:, Q:]
     row = row[:, :Q]
@@ -478,31 +484,42 @@
         for m in range(4)
     ]
     stat = jnp.concatenate(pieces + [jnp.zeros((4, Q), F32)], axis=0)
-    rounds = (
-        [other],
-        [z_peer(k)[1] for k in range(1, 8)],
-        [x_peer(k)[1] for k in range(1, 4)],
-        [y_peer(k)[1] for k in range(1, 4)],
-    )
-    at = 0
+    rounds = ([], [])
+    for k in range(1, 16):
+        to = (z + k % 8) % 8
+        rounds[0].append((y * 8 + (to % 2) * 4 + x, (to // 2) * 2 + (core + k // 8) % 2))
+        rounds[1].append((((y + k // 4) % 4) * 8 + z_lo * 4 + (x + k % 4) % 4, gy))
     stat_copies = []
     for r, peers in enumerate(rounds):
         stat_s[r] = stat
         now = [
-            remote(stat_s.at[r], stat_r.at[at + i], ts_sem.at[at + i], tr_sem.at[at + i], who)
+            remote(stat_s.at[r], stat_r.at[15 * r + i], ts_sem.at[15 * r + i], tr_sem.at[15 * r + i], who)
             for i, who in enumerate(peers)
         ]
         for copy in now:
             copy.start()
+        if r == 1:
+            out_grad = node_gradient()
         for copy in now:
             copy.wait_recv()
-        for i in range(len(peers)):
-            stat = stat + stat_r[at + i]
-        at += len(peers)
+        for i in range(15):
+            stat = stat + stat_r[15 * r + i]
         stat_copies += now
 
-    swap.wait_recv()
-    keep = jnp.where(core == 0, first, second)
+    taken = [
+        remote(swap_s.at[c], swap_r.at[c], ws_sem.at[c], wr_sem.at[c], (from_gx, z_hi * 2 + c))
+        for c in range(2)
+    ]
+    for c in range(2):
+
+        @pl.when(jnp.logical_or(from_gx != gx, core != c))
+        def _():
+            taken[c].wait_recv()
+
+    @pl.when(own_blk == gx)
+    def _():
+        stay.wait()
+
     scales = [
         lax.rsqrt(jnp.sum(stat[m : m + 1], axis=-1, keepdims=True) * (1.0 / SIZES[m]) + 1e-06)
         for m in range(4)
@@ -513,9 +530,8 @@
         scales[0],
         jnp.where(row < BOUNDS[1], scales[1], jnp.where(row < BOUNDS[2], scales[2], scales[3])),
     )
-    theirs = swap_r[...]
-    left = jnp.where(core == 0, keep, theirs) * scale
-    right = jnp.where(core == 0, theirs, keep) * scale
+    left = swap_r[0] * scale
+    right = swap_r[1] * scale
     for g in range(2):
         flat[pl.ds(g, 16, stride=4), :] = left[:, g * Q : (g + 1) * Q]
         flat[pl.ds(2 + g, 16, stride=4), :] = right[:, g * Q : (g + 1) * Q]
@@ -527,12 +543,26 @@
         def _():
             home[q].wait_send()
 
-    for copy in cores + early + late + sides + second_a + second_b + along + stat_copies:
+    for copy in cores + early + late + second + along + stat_copies:
         copy.wait_send()
-    swap.wait_send()
+    for c in range(2):
+
+        @pl.when(jnp.logical_or(own_blk != gx, core != c))
+        def _():
+            swap[c].wait_send()
+
     out_node.wait()
     out_edge.wait()
     out_grad.wait()
+
+
+def hand_over(*refs):
+    sem = refs[-1]
+    copies = [pltpu.make_async_copy(refs[i], refs[4 + i], sem.at[i]) for i in range(4)]
+    for copy in copies:
+        copy.start()
+    for copy in copies:
+        copy.wait()
 
 
 def on_device(
@@ -545,7 +575,6 @@
     b = functools.partial(pltpu.VMEM, dtype=BF16)
     f = functools.partial(pltpu.VMEM, dtype=F32)
     sem = lambda n: pltpu.SemaphoreType.DMA((n,))
-    one = pltpu.SemaphoreType.DMA
     scratch = [
         b((2, Q, D)), b((10, Q, D)), b((768, D)), b((3 * D, D)), b((D, D)), b((2 * D, D)), b((D, D)),
         b((H, D)), b((768, D)), b((4, 2, Q, D)), b((6, Q, Q)), b((6, Q, Q)),
@@ -554,22 +583,23 @@
         b((H, 2 * D)), b((H, D)), b((H, D)), f((6, Q, D)), b((4, 2, Q, D)), b((4, 2, Q, D)),
         b((H, D)), b((H, D)), b((768, D)),
         b((ROWS, H)), f((ROWS, H)), b((ROWS, H)),
-        b((8, 4, BLK, Q)), b((8, 4, BLK, Q)), b((3, 8, BLK, Q)), b((3, 2, 4, BLK, Q)),
+        b((8, 4, BLK, Q)), b((8, 4, BLK, Q)), b((3, 8, BLK, Q)), b((3, 8, BLK, Q)),
         b((4, 2, BLK, Q)), b((4, 2, BLK, Q)), b((3, 2, BLK, Q)), b((3, 2, BLK, Q)),
-        f((2, Q, H)), b((8, 32, H)), b((7, 32, H)), f((32, H)), f((16, H)), f((16, H)),
-        f((4, 8, Q)), f((14, 8, Q)), f((64, Q)),
+        f((2, Q, H)), b((8, 32, H)), b((7, 32, H)), f((32, H)), f((2, 16, H)), f((2, 16, H)),
+        f((2, 8, Q)), f((30, 8, Q)), f((64, Q)),
         sem(9), sem(3), sem(4), sem(4), sem(4), sem(4), sem(5), sem(5),
-        sem(6), sem(6), sem(3), sem(3), sem(3), sem(3), sem(3), sem(3),
-        sem(7), sem(7), one, one, sem(14), sem(14),
-    ]
-    nout, ngrad, egrad, wdir = pl.pallas_call(
+        sem(6), sem(6), sem(6), sem(6), sem(3), sem(3), sem(3), sem(3),
+        sem(7), sem(7), sem(2), sem(2), sem(30), sem(30),
+    ]
+    shapes = (
+        jax.ShapeDtypeStruct((H, D), BF16),
+        jax.ShapeDtypeStruct((H, D), BF16),
+        jax.ShapeDtypeStruct((768, D), BF16),
+        jax.ShapeDtypeStruct((56, Q), BF16),
+    )
+    results = pl.pallas_call(
         kernel,
-        out_shape=(
-            jax.ShapeDtypeStruct((H, D), BF16),
-            jax.ShapeDtypeStruct((H, D), BF16),
-            jax.ShapeDtypeStruct((768, D), BF16),
-            jax.ShapeDtypeStruct((56, Q), BF16),
-        ),
+        out_shape=shapes,
         in_specs=[smem] * 4 + [vmem] * 3 + [hbm] * 8,
         out_specs=(hbm, hbm, hbm, vmem),
         scratch_shapes=scratch,
@@ -578,12 +608,21 @@
         ),
         name="layer",
     )(
-        send_count, send_list, tile_recv, tile_send, tile_perm,
+        send_count, jnp.transpose(send_list, (0, 1, 3, 2)), tile_recv, tile_send,
+        jnp.transpose(tile_perm, (0, 2, 1, 3)),
         edge_b1.reshape(1, D), node_b1.reshape(1, D),
         node_latents.reshape(2, Q, D), edge_latents.reshape(768, D),
         edge_w1, edge_w2, node_w1, node_w2,
         node_cot.reshape(H, D), edge_cot.reshape(768, D),
     )
+    nout, ngrad, egrad, wdir = pl.pallas_call(
+        hand_over,
+        out_shape=shapes,
+        in_specs=[hbm] * 4,
+        out_specs=(hbm,) * 4,
+        scratch_shapes=[sem(4)],
+        name="hand_over",
+    )(*results)
     return (
         nout.reshape(1, 1, H, D),
         ngrad.reshape(1, 1, H, D),

time: 84.7 us -> 114 us (1.35)
  Pallas kernels: 76.3 us -> 113 us
  local copies, waits for them, and re-layouts: 7.51 us -> 0 us
    pallas_call x1 -> x2, Pallas kernels: 76.3 us -> 113 us  [the longest x1 71.6 us: on_device(): pl.pallas_call(kernel, out_shape=shapes, in_specs=[smem] * 4 + [vmem] * 3...]
    unnamed x10 -> x0, local copies, waits for them, and re-layouts: 7.51 us -> none
where the time goes in v2:
time: 114 us
  Pallas kernels  113 us (99%)
    pallas_call x1, Pallas kernels, on_device(): pl.pallas_call(kernel, out_shape=shapes, in_specs=[smem] * 4 + [vmem] * 3...  71.6 us
    pallas_call x1, Pallas kernels, on_device(): pl.pallas_call(hand_over, out_shape=shapes, in_specs=[hbm] * 4, out_specs...  41.3 us

profile of v2, /device:TPU:1, one launch (start us, length us, event | category | flops | bytes accessed | tf_op | source)
XLA Modules:
  0.0 113.5 jit_solution(18363040091290772661)
XLA Ops:
  0.6 71.6 %layer.1 = (bf16[256,512]{1,0:T(8,128)(2,1)}, bf16[256,512]{1,0:T(8,128)(2,1)}, bf16[768,512]{1,0:T(8,128)(2,1)}, bf16[56,128]{1,0:T(8,128)(2,1)}) custom-call(s32[1,1,4]{2,1,0:T(1,128)} %count_s.1, s32[1,1,2,4]{3,2,1,0:T(2,128)} %bitcast.19, s32[1,1,6]{2,1,0:T(1,128)} %recv_s.1, s32[1,1,6]{2,1,0:T(1,128)} %send_s.1, s32[1,6,1,128]{3,2,1,0:T(1,128)} %bitcast.16, ...), custom_call_target="tpu_custom_call" | custom-call | tf_op jit(solution)/shard_map/layer/pallas_call | solution.py:600
  72.2 41.3 %hand_over.1 = (bf16[256,512]{1,0:T(8,128)(2,1)}, bf16[256,512]{1,0:T(8,128)(2,1)}, bf16[768,512]{1,0:T(8,128)(2,1)}, bf16[56,128]{1,0:T(8,128)(2,1)}) custom-call(bf16[256,512]{1,0:T(8,128)(2,1)} %get-tuple-element.12.refs_0_, bf16[256,512]{1,0:T(8,128)(2,1)} %get-tuple-element.13.refs_1_, bf16[768,512]{1,0:T(8,128)(2,1)} %get-tuple-element.14.refs_2_, ...), custom_call_target="tpu_custom_call" | custom-call | tf_op jit(solution)/shard_map/hand_over/pallas_call | solution.py:618

commit v3 on v2

--- a/solution.py
+++ b/solution.py
@@ -178,12 +178,6 @@
         )
         return c
 
-    for q in range(4):
-
-        @pl.when(has[q])
-        def _():
-            halo[q].wait_send()
-
     lax.fori_loop(0, 3, before, 0)
     agg[...] = jnp.zeros_like(agg)
     for load in loads[3:]:
@@ -427,6 +421,14 @@
     for copy in along:
         copy.start()
 
+    for q in range(4):
+
+        @pl.when(has[q])
+        def _():
+            halo[q].wait_send()
+
+    for copy in cores + early + late + second:
+        copy.wait_send()
     for copy in along:
         copy.wait_recv()
     total = s3[z_lo * 4 + z_hi].astype(F32)
@@ -492,19 +494,15 @@
     stat_copies = []
     for r, peers in enumerate(rounds):
         stat_s[r] = stat
-        now = [
-            remote(stat_s.at[r], stat_r.at[15 * r + i], ts_sem.at[15 * r + i], tr_sem.at[15 * r + i], who)
-            for i, who in enumerate(peers)
-        ]
-        for copy in now:
-            copy.start()
+        for i, who in enumerate(peers):
+            remote(stat_s.at[r], stat_r.at[r, i], ts_sem.at[r], tr_sem.at[r], who).start()
+        everyone = remote(stat_r.at[r], stat_r.at[r], ts_sem.at[r], tr_sem.at[r], peers[0])
         if r == 1:
             out_grad = node_gradient()
-        for copy in now:
-            copy.wait_recv()
+        everyone.wait_recv()
         for i in range(15):
-            stat = stat + stat_r[15 * r + i]
-        stat_copies += now
+            stat = stat + stat_r[r, i]
+        stat_copies.append(everyone)
 
     taken = [
         remote(swap_s.at[c], swap_r.at[c], ws_sem.at[c], wr_sem.at[c], (from_gx, z_hi * 2 + c))
@@ -543,7 +541,7 @@
         def _():
             home[q].wait_send()
 
-    for copy in cores + early + late + second + along + stat_copies:
+    for copy in along + stat_copies:
         copy.wait_send()
     for c in range(2):
 
@@ -557,11 +555,15 @@
 
 
 def hand_over(*refs):
-    sem = refs[-1]
-    copies = [pltpu.make_async_copy(refs[i], refs[4 + i], sem.at[i]) for i in range(4)]
-    for copy in copies:
+    given, results, held, sem_in, sem_out = refs[:4], refs[4:8], refs[8:12], refs[12], refs[13]
+    into = [pltpu.make_async_copy(given[i], held[i], sem_in.at[i]) for i in range(4)]
+    out = [pltpu.make_async_copy(held[i], results[i], sem_out.at[i]) for i in range(4)]
+    for copy in into:
         copy.start()
-    for copy in copies:
+    for i in range(4):
+        into[i].wait()
+        out[i].start()
+    for copy in out:
         copy.wait()
 
 
@@ -586,10 +588,10 @@
         b((8, 4, BLK, Q)), b((8, 4, BLK, Q)), b((3, 8, BLK, Q)), b((3, 8, BLK, Q)),
         b((4, 2, BLK, Q)), b((4, 2, BLK, Q)), b((3, 2, BLK, Q)), b((3, 2, BLK, Q)),
         f((2, Q, H)), b((8, 32, H)), b((7, 32, H)), f((32, H)), f((2, 16, H)), f((2, 16, H)),
-        f((2, 8, Q)), f((30, 8, Q)), f((64, Q)),
+        f((2, 8, Q)), f((2, 15, 8, Q)), f((64, Q)),
         sem(9), sem(3), sem(4), sem(4), sem(4), sem(4), sem(5), sem(5),
         sem(6), sem(6), sem(6), sem(6), sem(3), sem(3), sem(3), sem(3),
-        sem(7), sem(7), sem(2), sem(2), sem(30), sem(30),
+        sem(7), sem(7), sem(2), sem(2), sem(2), sem(2),
     ]
     shapes = (
         jax.ShapeDtypeStruct((H, D), BF16),
@@ -620,7 +622,7 @@
         out_shape=shapes,
         in_specs=[hbm] * 4,
         out_specs=(hbm,) * 4,
-        scratch_shapes=[sem(4)],
+        scratch_shapes=[b((H, D)), b((H, D)), b((768, D)), b((56, Q)), sem(4), sem(4)],
         name="hand_over",
     )(*results)
     return (

time: 114 us -> 74.1 us (0.65)
  Pallas kernels: 113 us -> 73.3 us
    pallas_call x1, Pallas kernels: 41.3 us -> 2.25 us  [on_device(): pl.pallas_call(hand_over, out_shape=shapes, in_specs=[hbm] * 4, out_specs...]
where the time goes in v3:
time: 74.1 us; the launch traced here: 74 us
  Pallas kernels  73.3 us (99%)
    pallas_call x1, Pallas kernels, on_device(): pl.pallas_call(kernel, out_shape=shapes, in_specs=[smem] * 4 + [vmem] * 3...  71.1 us
    pallas_call x1, Pallas kernels, on_device(): pl.pallas_call(hand_over, out_shape=shapes, in_specs=[hbm] * 4, out_specs...  2.25 us

profile of v3, /device:TPU:1, one launch (start us, length us, event | category | flops | bytes accessed | tf_op | source)
XLA Modules:
  0.0 74.0 jit_solution(6358982408687011319)
XLA Ops:
  0.6 71.1 %layer.1 = (bf16[256,512]{1,0:T(8,128)(2,1)}, bf16[256,512]{1,0:T(8,128)(2,1)}, bf16[768,512]{1,0:T(8,128)(2,1)}, bf16[56,128]{1,0:T(8,128)(2,1)}) custom-call(s32[1,1,4]{2,1,0:T(1,128)} %count_s.1, s32[1,1,2,4]{3,2,1,0:T(2,128)} %bitcast.19, s32[1,1,6]{2,1,0:T(1,128)} %recv_s.1, s32[1,1,6]{2,1,0:T(1,128)} %send_s.1, s32[1,6,1,128]{3,2,1,0:T(1,128)} %bitcast.16, ...), custom_call_target="tpu_custom_call" | custom-call | tf_op jit(solution)/shard_map/layer/pallas_call | solution.py:602
  71.7 2.2 %hand_over.1 = (bf16[256,512]{1,0:T(8,128)(2,1)}, bf16[256,512]{1,0:T(8,128)(2,1)}, bf16[768,512]{1,0:T(8,128)(2,1)}, bf16[56,128]{1,0:T(8,128)(2,1)}) custom-call(bf16[256,512]{1,0:T(8,128)(2,1)} %get-tuple-element.12.refs_0_, bf16[256,512]{1,0:T(8,128)(2,1)} %get-tuple-element.13.refs_1_, bf16[768,512]{1,0:T(8,128)(2,1)} %get-tuple-element.14.refs_2_, ...), custom_call_target="tpu_custom_call" | custom-call | tf_op jit(solution)/shard_map/hand_over/pallas_call | solution.py:620

commit v4 on v3

--- a/solution.py
+++ b/solution.py
@@ -16,8 +16,7 @@
 ROWS = 7 * D
 CHIP_ROWS = 28
 BLK = 112
-NGROUP = 8
-EARLY = 5
+PARTS = ((4, 8), (0, 2), (2, 4))
 BOUNDS = (3 * D, 4 * D, 6 * D)
 SIZES = (3 * D * D, D * D, 2 * D * D, D * D)
 PIECES = ((4 * D, 3 * D), (3 * D, D), (0, D), (D, D), (2 * D, D))
@@ -63,12 +62,12 @@
     nodes_h, edges_h, ew1_h, ew2_h, nw1_h, nw2_h, cotn_h, cote_h,
     nout_h, ngrad_h, egrad_h, wdir,
     loc, ext, edges, ew1, ew2, nw1, nw2, cotn, cote, pack, pt, pm,
-    hr, hs, aff, hid, msg, einv, agg, gagg, owned, gea, geap, gel_p,
+    edges_t, hr_t, loc_t, hr, hs, aff, hid, msg, einv, agg, gagg, owned, gea, geap, gel_p,
     nin, gna_p, gnl_p, xs, hret, ret, nout, ngrad, egrad,
-    gsend, gown, grecv, g1a, g1b, r1a, r1b, g2a, g2b, r2a, r2b,
+    gsend, gown, grecv, g1a, g1b, r1a, r1b, via_a, via_b, g2a, g2b, r2a, r2b,
     g3, s3, r3, fin, swap_s, swap_r, stat_s, stat_r, flat,
     in_sem, out_sem, hs_sem, hr_sem, bs_sem, br_sem, cs_sem, cr_sem,
-    as_sem, ar_sem, ys_sem, yr_sem, a2s_sem, a2r_sem, b2s_sem, b2r_sem,
+    ms_sem, mr_sem, ns_sem, nr_sem, as_sem, ar_sem, ys_sem, yr_sem, a2s_sem, a2r_sem, b2s_sem, b2r_sem,
     zs_sem, zr_sem, ws_sem, wr_sem, ts_sem, tr_sem,
 ):
     gx = lax.axis_index("gx")
@@ -116,22 +115,23 @@
             )
         )
     ]
-    for load in loads:
-        load.start()
-
+    loads[0].start()
     barrier = pltpu.get_barrier_semaphore()
     fixed = [other]
     fixed += [x_peer(k)[1] for k in range(1, 4)]
     fixed += [y_peer(k)[1] for k in range(1, 4)]
     fixed += [z_peer(k)[1] for k in range(1, 8)]
+    for peer in reversed(fixed):
+        pl.semaphore_signal(barrier, inc=1, device_id=peer, device_id_type=MESH)
+
     for q in range(4):
 
         @pl.when(has[q])
         def _():
             pl.semaphore_signal(barrier, inc=1, device_id=nxt[q], device_id_type=MESH)
 
-    for peer in fixed:
-        pl.semaphore_signal(barrier, inc=1, device_id=peer, device_id_type=MESH)
+    for load in loads[1:]:
+        load.start()
 
     loads[0].wait()
     for q in range(4):
@@ -179,6 +179,16 @@
         return c
 
     lax.fori_loop(0, 3, before, 0)
+
+    def turn(i, c):
+        rows = pl.ds(pl.multiple_of(i * H, H), H)
+        edges_t[:, rows] = edges[rows, :].T
+        hr_t[:, rows] = hr[rows, :].T
+        return c
+
+    lax.fori_loop(0, 3, turn, 0)
+    for b in range(2):
+        loc_t[:, pl.ds(b * Q, Q)] = loc[b].T
     agg[...] = jnp.zeros_like(agg)
     for load in loads[3:]:
         load.wait()
@@ -251,10 +261,19 @@
 
         lax.fori_loop(0, blocks, one, 0)
 
+    def outer_turned(left, right, base, blocks):
+        def one(j, c):
+            j = pl.multiple_of(j * H, H)
+            put(base + j, dot(left[pl.ds(j, H), :], right[...]))
+            return c
+
+        lax.fori_loop(0, blocks, one, 0)
+
     geap[pl.ds(0, H), :] = nhid
     outer_rows = geap.at[pl.ds(0, H), :]
     outer(outer_rows, gnl_p, 6 * D, 2)
-    outer(nin, gna_p, 4 * D, 4)
+    outer_turned(loc_t, gna_p, 4 * D, 2)
+    outer(nin.at[:, pl.ds(D, D)], gna_p, 5 * D, 2)
     cores[0].start()
 
     def backward(i, c):
@@ -285,40 +304,71 @@
 
         lax.fori_loop(lo, hi, one, 0)
 
-    early, late = [], []
-    for got, lo, n, sem in ((early, EARLY, NGROUP - EARLY, 0), (late, 0, EARLY, 3)):
-        for k in range(1, 4):
-            to, who = x_peer(k)
-            got.append(
-                remote(
-                    g1a.at[pl.ds(lo, n), to], r1a.at[k - 1, pl.ds(lo, n)],
-                    as_sem.at[sem + k - 1], ar_sem.at[sem + k - 1], who,
-                )
-            )
-            to, who = y_peer(k)
-            got.append(
-                remote(
-                    g1b.at[pl.ds(lo, n), to], r1b.at[k - 1, pl.ds(lo, n)],
-                    ys_sem.at[sem + k - 1], yr_sem.at[sem + k - 1], who,
-                )
-            )
-
-    cores[0].wait_recv()
-    pair_sum(4 * EARLY, 32)
-    for copy in early:
-        copy.start()
-
-    outer(edges, geap, 0, 2)
+    ahead, right = x_peer(1)
+    behind, left = x_peer(3)
+    above, upper = y_peer(1)
+    below, lower = y_peer(3)
+    x_far, y_far = (x + 2) % 4, (y + 2) % 4
+    through, first = [], []
+    for p, (lo, hi) in enumerate(PARTS):
+        n = (hi - lo) // 2
+        one, two, i = pl.ds(lo, n), pl.ds(lo + n, n), 2 * p
+        through.append(
+            [
+                remote(g1a.at[one, x_far], via_a.at[one], ms_sem.at[i], mr_sem.at[i], right),
+                remote(g1b.at[one, y_far], via_b.at[one], ns_sem.at[i], nr_sem.at[i], upper),
+                remote(g1a.at[two, x_far], via_a.at[two], ms_sem.at[i + 1], mr_sem.at[i + 1], left),
+                remote(g1b.at[two, y_far], via_b.at[two], ns_sem.at[i + 1], nr_sem.at[i + 1], lower),
+            ]
+        )
+        both = pl.ds(lo, hi - lo)
+        first.append(
+            [
+                remote(g1a.at[both, ahead], r1a.at[0, both], as_sem.at[i], ar_sem.at[i], right),
+                remote(g1b.at[both, above], r1b.at[0, both], ys_sem.at[i], yr_sem.at[i], upper),
+                remote(g1a.at[both, behind], r1a.at[1, both], as_sem.at[i + 1], ar_sem.at[i + 1], left),
+                remote(g1b.at[both, below], r1b.at[1, both], ys_sem.at[i + 1], yr_sem.at[i + 1], lower),
+            ]
+        )
+
+    def first_half(p, needed):
+        for copy in needed:
+            copy.wait_recv()
+        pair_sum(4 * PARTS[p][0], 4 * PARTS[p][1])
+        for copy in through[p]:
+            copy.start()
+
+    def second_half(p):
+        lo, hi = PARTS[p]
+        mid = (lo + hi) // 2
+        for copy in through[p]:
+            copy.wait_recv()
+
+        def merge(x_to, y_to):
+            def one(g, c):
+                g1a[g, x_to] = (g1a[g, x_to].astype(F32) + via_a[g].astype(F32)).astype(BF16)
+                g1b[g, y_to] = (g1b[g, y_to].astype(F32) + via_b[g].astype(F32)).astype(BF16)
+                return c
+
+            return one
+
+        lax.fori_loop(lo, mid, merge(ahead, above), 0)
+        lax.fori_loop(mid, hi, merge(behind, below), 0)
+        for copy in first[p]:
+            copy.start()
+
+    outer_turned(edges_t, geap, 0, 2)
     cores[2].start()
-    outer(hr, geap, D, 2)
+    first_half(0, cores[:2])
+    outer_turned(hr_t, geap, D, 2)
     cores[3].start()
     outer(hs, geap, 2 * D, 2)
     cores[4].start()
-    for copy in cores[1:]:
-        copy.wait_recv()
-    pair_sum(0, 4 * EARLY)
-    for copy in late:
-        copy.start()
+    second_half(0)
+    first_half(1, cores[2:4])
+    first_half(2, cores[4:])
+    second_half(1)
+    second_half(2)
 
     def inputs(i, c):
         rows = pl.ds(i * H, H)
@@ -356,7 +406,7 @@
     home = [
         remote(hret.at[q], ret.at[q], bs_sem.at[q], br_sem.at[q], back[q]) for q in range(4)
     ]
-    for q in range(4):
+    for q in range(2, 4):
 
         @pl.when(came[q])
         def _():
@@ -370,21 +420,19 @@
 
     def sum_first(g, c):
         total = g1a[g, x].astype(F32)
-        for k in range(3):
+        for k in range(2):
             total += r1a[k, g].astype(F32)
         g2a[(g + x) % 4, g // 4] = total.astype(BF16)
         total = g1b[g, y].astype(F32)
-        for k in range(3):
+        for k in range(2):
             total += r1b[k, g].astype(F32)
         g2b[(y + 8 - g) % 4, g // 4] = total.astype(BF16)
         return c
 
-    for copy in early:
-        copy.wait_recv()
-    lax.fori_loop(EARLY, NGROUP, sum_first, 0)
-    for copy in late:
-        copy.wait_recv()
-    lax.fori_loop(0, EARLY, sum_first, 0)
+    for p, (lo, hi) in enumerate(PARTS):
+        for copy in first[p]:
+            copy.wait_recv()
+        lax.fori_loop(lo, hi, sum_first, 0)
     second = []
     for k in range(1, 4):
         to, who = y_peer(k)
@@ -421,13 +469,19 @@
     for copy in along:
         copy.start()
 
+    for q in range(2):
+
+        @pl.when(came[q])
+        def _():
+            home[q].start()
+
     for q in range(4):
 
         @pl.when(has[q])
         def _():
             halo[q].wait_send()
 
-    for copy in cores + early + late + second:
+    for copy in cores + through[0] + through[1] + through[2] + first[0] + first[1] + first[2] + second:
         copy.wait_send()
     for copy in along:
         copy.wait_recv()
@@ -486,22 +540,29 @@
         for m in range(4)
     ]
     stat = jnp.concatenate(pieces + [jnp.zeros((4, Q), F32)], axis=0)
-    rounds = ([], [])
-    for k in range(1, 16):
-        to = (z + k % 8) % 8
-        rounds[0].append((y * 8 + (to % 2) * 4 + x, (to // 2) * 2 + (core + k // 8) % 2))
-        rounds[1].append((((y + k // 4) % 4) * 8 + z_lo * 4 + (x + k % 4) % 4, gy))
+    rounds = (
+        [other],
+        [z_peer(k)[1] for k in range(1, 8)],
+        [
+            (((y + k // 4) % 4) * 8 + z_lo * 4 + (x + k % 4) % 4, gy)
+            for k in (5, 7, 13, 15, 6, 9, 11, 14, 10, 1, 3, 4, 12, 2, 8)
+        ],
+    )
     stat_copies = []
+    at = 0
     for r, peers in enumerate(rounds):
+        n = len(peers)
         stat_s[r] = stat
         for i, who in enumerate(peers):
-            remote(stat_s.at[r], stat_r.at[r, i], ts_sem.at[r], tr_sem.at[r], who).start()
-        everyone = remote(stat_r.at[r], stat_r.at[r], ts_sem.at[r], tr_sem.at[r], peers[0])
-        if r == 1:
+            remote(stat_s.at[r], stat_r.at[at + i], ts_sem.at[r], tr_sem.at[r], who).start()
+        got = stat_r.at[pl.ds(at, n)]
+        everyone = remote(got, got, ts_sem.at[r], tr_sem.at[r], peers[0])
+        if r == 2:
             out_grad = node_gradient()
         everyone.wait_recv()
-        for i in range(15):
-            stat = stat + stat_r[r, i]
+        for i in range(n):
+            stat = stat + stat_r[at + i]
+        at += n
         stat_copies.append(everyone)
 
     taken = [
@@ -580,18 +641,19 @@
     scratch = [
         b((2, Q, D)), b((10, Q, D)), b((768, D)), b((3 * D, D)), b((D, D)), b((2 * D, D)), b((D, D)),
         b((H, D)), b((768, D)), b((4, 2, Q, D)), b((6, Q, Q)), b((6, Q, Q)),
+        b((D, 768)), b((D, 768)), b((D, H)),
         b((768, D)), b((768, D)), f((768, D)), b((768, D)), f((768, D)), f((768, 1)),
         f((2, Q, D)), f((2, Q, D)), f((2, Q, D)), b((768, D)), b((768, D)), b((768, D)),
         b((H, 2 * D)), b((H, D)), b((H, D)), f((6, Q, D)), b((4, 2, Q, D)), b((4, 2, Q, D)),
         b((H, D)), b((H, D)), b((768, D)),
         b((ROWS, H)), f((ROWS, H)), b((ROWS, H)),
-        b((8, 4, BLK, Q)), b((8, 4, BLK, Q)), b((3, 8, BLK, Q)), b((3, 8, BLK, Q)),
+        b((8, 4, BLK, Q)), b((8, 4, BLK, Q)), b((2, 8, BLK, Q)), b((2, 8, BLK, Q)), b((8, BLK, Q)), b((8, BLK, Q)),
         b((4, 2, BLK, Q)), b((4, 2, BLK, Q)), b((3, 2, BLK, Q)), b((3, 2, BLK, Q)),
         f((2, Q, H)), b((8, 32, H)), b((7, 32, H)), f((32, H)), f((2, 16, H)), f((2, 16, H)),
-        f((2, 8, Q)), f((2, 15, 8, Q)), f((64, Q)),
+        f((3, 8, Q)), f((23, 8, Q)), f((64, Q)),
         sem(9), sem(3), sem(4), sem(4), sem(4), sem(4), sem(5), sem(5),
-        sem(6), sem(6), sem(6), sem(6), sem(3), sem(3), sem(3), sem(3),
-        sem(7), sem(7), sem(2), sem(2), sem(2), sem(2),
+        sem(6), sem(6), sem(6), sem(6), sem(6), sem(6), sem(6), sem(6), sem(3), sem(3), sem(3), sem(3),
+        sem(7), sem(7), sem(2), sem(2), sem(3), sem(3),
     ]
     shapes = (
         jax.ShapeDtypeStruct((H, D), BF16),

time: 74.1 us -> 73.9 us (level); the launches traced: 74 us -> 73 us
  Pallas kernels: 73.3 us -> 72.3 us
    pallas_call x1, Pallas kernels: 71.1 us -> 70.1 us  [on_device(): pl.pallas_call(kernel, out_shape=shapes, in_specs=[smem] * 4 + [vmem] * 3...]
where the time goes in v4:
time: 73.9 us; the launch traced here: 73 us
  Pallas kernels  72.3 us (98%)
    pallas_call x1, Pallas kernels, on_device(): pl.pallas_call(kernel, out_shape=shapes, in_specs=[smem] * 4 + [vmem] * 3...  70.1 us
    pallas_call x1, Pallas kernels, on_device(): pl.pallas_call(hand_over, out_shape=shapes, in_specs=[hbm] * 4, out_specs...  2.25 us

profile of v4, /device:TPU:1, one launch (start us, length us, event | category | flops | bytes accessed | tf_op | source)
XLA Modules:
  0.0 73.0 jit_solution(2533930755365157741)
XLA Ops:
  0.6 70.1 %layer.1 = (bf16[256,512]{1,0:T(8,128)(2,1)}, bf16[256,512]{1,0:T(8,128)(2,1)}, bf16[768,512]{1,0:T(8,128)(2,1)}, bf16[56,128]{1,0:T(8,128)(2,1)}) custom-call(s32[1,1,4]{2,1,0:T(1,128)} %count_s.1, s32[1,1,2,4]{3,2,1,0:T(2,128)} %bitcast.19, s32[1,1,6]{2,1,0:T(1,128)} %recv_s.1, s32[1,1,6]{2,1,0:T(1,128)} %send_s.1, s32[1,6,1,128]{3,2,1,0:T(1,128)} %bitcast.16, ...), custom_call_target="tpu_custom_call" | custom-call | tf_op jit(solution)/shard_map/layer/pallas_call | solution.py:664
  70.7 2.2 %hand_over.1 = (bf16[256,512]{1,0:T(8,128)(2,1)}, bf16[256,512]{1,0:T(8,128)(2,1)}, bf16[768,512]{1,0:T(8,128)(2,1)}, bf16[56,128]{1,0:T(8,128)(2,1)}) custom-call(bf16[256,512]{1,0:T(8,128)(2,1)} %get-tuple-element.12.refs_0_, bf16[256,512]{1,0:T(8,128)(2,1)} %get-tuple-element.13.refs_1_, bf16[768,512]{1,0:T(8,128)(2,1)} %get-tuple-element.14.refs_2_, ...), custom_call_target="tpu_custom_call" | custom-call | tf_op jit(solution)/shard_map/hand_over/pallas_call | solution.py:682
